TPU v7x, 32 devices: a whole 2x2x4 slice. The times are simulated.
32 devices in a mesh: head: 2 (over x), blk: 16 (over z, y, core).
Axes of the slice: x: 2, y: 2, z: 4, core: 2. Of those that a mesh axis runs over, the one named last changes fastest.
Arguments:
- tokens: bfloat16 [4096, 768], P(('blk', 'head')), may hold values from -6 to 6
- cotangent: bfloat16 [4096, 768], P(('blk', 'head')), may hold values from -6 to 6
- prev_logits: float32 [4096, 12], P(('blk', 'head')), may hold values from -6 to 6
- routes: int32 [4096, 2], P(('blk', 'head')), may hold values from 0 to 11, all different within a row; in each aligned block of 128 rows (0 to 127, 128 to 255, ...) at most 24 rows name the same one
- lengths: int32 [2], replicated, may hold values from 512 to 2048, as said below
- w_qkv: bfloat16 [768, 2304], P(('head', 'blk')), may hold values from -0.21875 to 0.21875
- w_out: bfloat16 [768, 768], P(('head', 'blk')), may hold values from -3.5 to 3.5
- w_router: bfloat16 [768, 12], P(('head', 'blk')), may hold values from -0.109375 to 0.109375
- w_const: bfloat16 [768, 4], P(('head', 'blk')), may hold values from -0.21875 to 0.21875
- const_vec: bfloat16 [768, 2], P(('head', 'blk')), may hold values from -5 to 5
- norm_gains: bfloat16 [768, 2], P(('head', 'blk')), may hold values from 0.5 to 1.5
- gate_mix: float32 [12, 12], replicated, may hold values from -0.875 to 0.875
- expert_weights: bfloat16 [2048, 8, 3, 768], P('blk', 'head')
Outputs:
- output: bfloat16 [4096, 768], P(('blk', 'head'))
- aux_loss: float32 [], replicated
- d_tokens: bfloat16 [4096, 768], P(('blk', 'head'))
- g_qkv: float32 [768, 2304], P(('head', 'blk'))
- g_out: float32 [768, 768], P(('head', 'blk'))
- g_router: float32 [768, 12], P(('head', 'blk'))
- g_const: float32 [768, 4], P(('head', 'blk'))
- g_vector: float32 [768, 2], P(('head', 'blk'))
- g_gains: float32 [768, 2], P(('head', 'blk'))
- g_mix: float32 [12, 12], replicated
- g_experts: float32 [2048, 8, 3, 768], P('blk', 'head')
Inputs may be any that keep to these rules, and one draw needn't show every extreme that they name: `routes`: in each aligned block of 128 rows (the rows of one device), no expert is named by more than 24 rows; the two experts of a row differ. `lengths`: some slot's length is exactly 2048 in every draw.
All inputs are finite; a program needn't handle non-finite values.
Results may differ from a plain program's by a relative error of at most 0.015.
Values may be sent and summed in bfloat16 or wider, within the bound.
A program may use at most 256 MiB of HBM per device.

v0:
```python
from functools import partial
import math

import jax
import jax.numpy as jnp
from jax import lax
from jax.sharding import PartitionSpec as P

HEADS = 12
HD = 64
CAP = 24


eps = 1e-06
aux_weight = 0.01
highest = lax.Precision.HIGHEST
masked_score = -1e30


def shifted(block, axis, distance):
    devices = range(lax.axis_size(axis))
    route = [(i - distance, i) for i in devices if i - distance in devices]
    return lax.ppermute(block, axis, route)


def for_sending(x):
    return jax.tree.map(lambda a: a.astype(jnp.bfloat16) if a.dtype == jnp.float32 else a, x)


def rms_norm(values, gain_vector):
    return values * lax.rsqrt(jnp.mean(values * values, axis=-1, keepdims=True) + eps) * gain_vector


def rotary(values, positions, turn_sign):
    half_width = values.shape[-1] // 2
    frequency = jnp.exp(
        jnp.arange(half_width, dtype=jnp.float32) * (-2.0 * math.log(10000.0) / values.shape[-1])
    )
    angles = positions.astype(jnp.float32)[:, None] * frequency[None, :]
    cosine = jnp.cos(angles)[:, None, :]
    sine_part = turn_sign * jnp.sin(angles)[:, None, :]
    first_half = values[..., :half_width]
    second_half = values[..., half_width:]
    return jnp.concatenate(
        [
            first_half * cosine - second_half * sine_part,
            second_half * cosine + first_half * sine_part,
        ],
        axis=-1,
    )


def slot_lengths(slot_ids, lengths):
    slot_table = jnp.arange(lengths.shape[0], dtype=jnp.int32)
    return jnp.sum(jnp.where(slot_ids[:, None] == slot_table[None, :], lengths[None, :], 0), axis=1)


def allowed_mask(query_ids, key_ids, slot_size, lengths):
    query_slot = query_ids // slot_size
    key_slot = key_ids // slot_size
    query_pos = query_ids - query_slot * slot_size
    key_pos = key_ids - key_slot * slot_size
    key_live = (key_pos < slot_lengths(key_slot, lengths)) & (key_ids >= 0)
    return (
        (query_slot[:, None] == key_slot[None, :])
        & (key_pos[None, :] <= query_pos[:, None])
        & key_live[None, :]
    )


def masked_scores(query_block, key_head, query_ids, key_ids, slot_size, lengths):
    scores = lax.dot_general(
        query_block, key_head, (((1,), (1,)), ((), ())), preferred_element_type=jnp.float32
    ) * HD ** (-0.5)
    return jnp.where(allowed_mask(query_ids, key_ids, slot_size, lengths), scores, masked_score)


def attend_forward(queries, key_all, value_all, query_ids, key_ids, slot_size, lengths):
    head_total = queries.shape[1] // HD

    def one_head(head_index):
        query_head = lax.dynamic_slice_in_dim(queries, head_index * HD, HD, 1)
        key_head = lax.dynamic_slice_in_dim(key_all, head_index * HD, HD, 1)
        value_head = lax.dynamic_slice_in_dim(value_all, head_index * HD, HD, 1)
        scores = masked_scores(query_head, key_head, query_ids, key_ids, slot_size, lengths)
        row_max = jnp.max(scores, axis=1, keepdims=True)
        weights = jnp.exp(scores - row_max)
        row_total = jnp.sum(weights, axis=1, keepdims=True)
        probs_low = (weights / row_total).astype(jnp.bfloat16)
        head_outputs = [jnp.dot(probs_low, value_head, preferred_element_type=jnp.float32)]
        log_parts = [row_max[:, 0] + jnp.log(row_total[:, 0])]
        return (jnp.concatenate(head_outputs, axis=0), jnp.concatenate(log_parts, axis=0))

    head_outputs, log_sums = lax.map(one_head, jnp.arange(head_total, dtype=jnp.int32))
    return (head_outputs.transpose(1, 0, 2).reshape(queries.shape[0], queries.shape[1]), log_sums)


def attend_backward(
    queries, key_all, value_all, out_grads, log_sums, query_ids, key_ids, slot_size, lengths
):
    head_total = queries.shape[1] // HD
    block_rows = min(512, queries.shape[0])

    def one_head(head_index):
        query_head = lax.dynamic_slice_in_dim(queries, head_index * HD, HD, 1)
        key_head = lax.dynamic_slice_in_dim(key_all, head_index * HD, HD, 1)
        value_head = lax.dynamic_slice_in_dim(value_all, head_index * HD, HD, 1)
        grad_head = lax.dynamic_slice_in_dim(out_grads, head_index * HD, HD, 1)
        log_head = lax.dynamic_index_in_dim(log_sums, head_index, 0, keepdims=False)
        key_grad = jnp.zeros(key_head.shape, jnp.float32)
        value_grad = jnp.zeros(value_head.shape, jnp.float32)
        grad_block = grad_head[0:block_rows]
        scores = masked_scores(query_head, key_head, query_ids, key_ids, slot_size, lengths)
        probs = jnp.exp(scores - log_head[0:block_rows][:, None])
        probs_low = probs.astype(jnp.bfloat16)
        prob_grads = lax.dot_general(
            grad_block, value_head, (((1,), (1,)), ((), ())), preferred_element_type=jnp.float32
        )
        row_inner = jnp.sum(probs * prob_grads, axis=1, keepdims=True)
        score_grads = (probs * (prob_grads - row_inner)).astype(jnp.bfloat16)
        query_parts = [
            jnp.dot(score_grads, key_head, preferred_element_type=jnp.float32) * HD ** (-0.5)
        ]
        key_grad = key_grad + lax.dot_general(
            score_grads, query_head, (((0,), (0,)), ((), ())), preferred_element_type=jnp.float32
        ) * HD ** (-0.5)
        value_grad = value_grad + lax.dot_general(
            probs_low, grad_block, (((0,), (0,)), ((), ())), preferred_element_type=jnp.float32
        )
        return (jnp.concatenate(query_parts, axis=0), key_grad, value_grad)

    query_grad, key_grad, value_grad = lax.map(one_head, jnp.arange(head_total, dtype=jnp.int32))
    return (
        query_grad.transpose(1, 0, 2).reshape(queries.shape[0], queries.shape[1]),
        key_grad.transpose(1, 0, 2).reshape(key_all.shape[0], key_all.shape[1]),
        value_grad.transpose(1, 0, 2).reshape(value_all.shape[0], value_all.shape[1]),
    )


def fetch_prev(key_heads, value_heads, span_count):
    key_parts = [key_heads]
    value_parts = [value_heads]
    for offset in range(1, span_count):
        arrived = shifted((key_heads, value_heads), "blk", offset)
        key_parts.append(arrived[0])
        value_parts.append(arrived[1])
    return (jnp.concatenate(key_parts, axis=0), jnp.concatenate(value_parts, axis=0))


def router_probs(normed, router_w, mixing, prev_scores):
    logits = jnp.dot(normed, router_w, precision=highest) + jnp.dot(
        prev_scores, mixing, precision=highest
    )
    return jax.nn.softmax(logits, axis=-1)


def branch_sum(router_prob, normed, const_w, vector_w, outputs_pair, choose, live_rows, real_count):
    gate_values = jnp.sum(choose * router_prob[:, None, :], axis=-1)
    expert_share = jnp.sum(choose * gate_values[:, :, None], axis=1) * live_rows[:, None]
    routed = jnp.sum(gate_values[:, :, None] * outputs_pair, axis=1)
    routed = routed + expert_share[:, real_count + 1 : real_count + 2] * normed
    const_count = vector_w.shape[1]
    const_mix = jax.nn.softmax(
        jnp.dot(normed, const_w, precision=highest).reshape(normed.shape[0], const_count, 2),
        axis=-1,
    )
    for const_index in range(const_count):
        const_out = (
            const_mix[:, const_index, 0:1] * normed
            + const_mix[:, const_index, 1:2] * vector_w[:, const_index][None, :]
        )
        routed = (
            routed
            + expert_share[:, real_count + 2 + const_index : real_count + 3 + const_index]
            * const_out
        )
    return routed


def on_device(
    tokens,
    cotangent,
    prev_logits,
    routes,
    lengths,
    w_qkv,
    w_out,
    w_router,
    w_const,
    const_vec,
    norm_gains,
    gate_mix,
    expert_weights,
):
    tok_dev = tokens.shape[0]
    model_width = tokens.shape[1]
    head_count = lax.axis_size("head")
    blk_count = lax.axis_size("blk")
    span_count = max(8, min(blk_count // 4, 8192 // (head_count * tok_dev)) * min(1, tok_dev // 64))
    head_index = lax.axis_index("head")
    blk_index = lax.axis_index("blk")
    slot_size = span_count * head_count * tok_dev
    tok_blk = head_count * tok_dev
    qkv_w, out_w, router_w, const_w, vector_w, gain_pair = (
        lax.all_gather(w_qkv, ("head", "blk"), axis=0, tiled=True),
        lax.all_gather(w_out, ("head", "blk"), axis=0, tiled=True),
        lax.all_gather(w_router, ("head", "blk"), axis=0, tiled=True),
        lax.all_gather(w_const, ("head", "blk"), axis=0, tiled=True),
        lax.all_gather(const_vec, ("head", "blk"), axis=0, tiled=True),
        lax.all_gather(norm_gains, ("head", "blk"), axis=0, tiled=True),
    )
    gain_pair = gain_pair.astype(jnp.float32)
    row_ids = (blk_index * head_count + head_index) * tok_dev + jnp.arange(tok_dev, dtype=jnp.int32)
    slot_ids = row_ids // slot_size
    positions = row_ids - slot_ids * slot_size
    live_rows = (positions < slot_lengths(slot_ids, lengths)).astype(jnp.float32)
    inputs = tokens.astype(jnp.float32)
    normed_one, norm_one_back = jax.vjp(rms_norm, inputs, gain_pair[:, 0])
    normed_one_low = normed_one.astype(jnp.bfloat16)
    projected = jnp.dot(normed_one_low, qkv_w, preferred_element_type=jnp.float32).reshape(
        tok_dev, 3, HEADS, HD
    )
    query_send = (
        rotary(projected[:, 0], positions, 1.0).astype(jnp.bfloat16).reshape(tok_dev, model_width)
    )
    key_send = (
        rotary(projected[:, 1], positions, 1.0).astype(jnp.bfloat16).reshape(tok_dev, model_width)
    )
    value_send = projected[:, 2].astype(jnp.bfloat16).reshape(tok_dev, model_width)
    query_heads, key_heads, value_heads = (
        lax.all_to_all(query_send, "head", split_axis=1, concat_axis=0, tiled=True),
        lax.all_to_all(key_send, "head", split_axis=1, concat_axis=0, tiled=True),
        lax.all_to_all(value_send, "head", split_axis=1, concat_axis=0, tiled=True),
    )
    blk_rows = blk_index * tok_blk + jnp.arange(tok_blk, dtype=jnp.int32)
    blk_pos = blk_rows - blk_rows // slot_size * slot_size
    key_ids = jnp.concatenate([blk_rows - offset * tok_blk for offset in range(span_count)], axis=0)
    key_all, value_all = fetch_prev(key_heads, value_heads, span_count)
    attended, log_sums = attend_forward(
        query_heads, key_all, value_all, blk_rows, key_ids, slot_size, lengths
    )
    attended_tok = lax.all_to_all(
        attended.astype(jnp.bfloat16), "head", split_axis=0, concat_axis=1, tiled=True
    )
    residual = inputs + jnp.dot(attended_tok, out_w, preferred_element_type=jnp.float32)
    normed_two, norm_two_back = jax.vjp(rms_norm, residual, gain_pair[:, 1])
    normed_two_low = normed_two.astype(jnp.bfloat16)
    normed_two_f = normed_two_low.astype(jnp.float32)
    router_prob, router_back = jax.vjp(
        partial(router_probs, prev_scores=prev_logits),
        normed_two_f,
        router_w.astype(jnp.float32),
        gate_mix,
    )
    expert_count = router_w.shape[1]
    real_count = expert_weights.shape[1] * head_count
    choose = (
        routes[:, :, None] == jnp.arange(expert_count, dtype=jnp.int32)[None, None, :]
    ).astype(jnp.float32)
    count_local = jnp.sum(jnp.sum(choose, axis=1) * live_rows[:, None], axis=0)
    prob_local = jnp.sum(router_prob * live_rows[:, None], axis=0)
    count_all, prob_all = lax.psum((count_local, prob_local), ("head", "blk"))
    live_total = jnp.sum(lengths).astype(jnp.float32)
    fraction = count_all / (2.0 * live_total)
    aux_loss = expert_count * jnp.sum(fraction * (prob_all / live_total))
    gate_values = jnp.sum(choose * router_prob[:, None, :], axis=-1)
    out_grad = live_rows[:, None] * cotangent.astype(jnp.float32)
    assigned = routes.reshape(-1)
    live_pairs = jnp.repeat(live_rows, 2)
    is_real = (assigned < real_count) & (live_pairs > 0)
    onehot = (
        (assigned[:, None] == jnp.arange(real_count, dtype=jnp.int32)[None, :]) & is_real[:, None]
    ).astype(jnp.int32)
    slot_rank = jnp.sum((jnp.cumsum(onehot, axis=0) - onehot) * onehot, axis=1)
    target = jnp.where(is_real, assigned * CAP + slot_rank, real_count * CAP)
    source = (
        jnp.full((real_count * CAP + 1,), 2 * tok_dev, jnp.int32)
        .at[target]
        .set(jnp.arange(2 * tok_dev, dtype=jnp.int32))[: real_count * CAP]
    )
    zero_row = jnp.zeros((1, model_width), jnp.bfloat16)
    send_rows = jnp.concatenate([normed_two_low, zero_row], axis=0)[source // 2].reshape(
        real_count, CAP, model_width
    )
    pair_grads = (gate_values.reshape(-1, 1) * jnp.repeat(out_grad, 2, axis=0)).astype(jnp.bfloat16)
    send_grads = jnp.concatenate([pair_grads, zero_row], axis=0)[source].reshape(
        real_count, CAP, model_width
    )
    expert_in, expert_cot = (
        lax.all_to_all(send_rows, "head", split_axis=0, concat_axis=1, tiled=True),
        lax.all_to_all(send_grads, "head", split_axis=0, concat_axis=1, tiled=True),
    )
    weight_piece = lax.all_gather(expert_weights, "blk", axis=0, tiled=True)
    gate_w = weight_piece[:, :, 0, :]
    up_w = weight_piece[:, :, 1, :]
    down_w = weight_piece[:, :, 2, :]
    gate_part = jnp.einsum("esd,ned->esn", expert_in, gate_w, preferred_element_type=jnp.float32)
    up_part = jnp.einsum("esd,ned->esn", expert_in, up_w, preferred_element_type=jnp.float32)
    sigmoid_part = jax.nn.sigmoid(gate_part)
    silu_part = gate_part * sigmoid_part
    hidden = (silu_part * up_part).astype(jnp.bfloat16)
    out_sum = jnp.einsum("esn,ned->esd", hidden, down_w, preferred_element_type=jnp.float32)
    hidden_grad = jnp.einsum("esd,ned->esn", expert_cot, down_w, preferred_element_type=jnp.float32)
    gate_grad = (
        hidden_grad * up_part * (sigmoid_part * (1.0 + gate_part * (1.0 - sigmoid_part)))
    ).astype(jnp.bfloat16)
    up_grad = (hidden_grad * silu_part).astype(jnp.bfloat16)
    in_grad = jnp.einsum("esn,ned->esd", gate_grad, gate_w, preferred_element_type=jnp.float32)
    in_grad = in_grad + jnp.einsum(
        "esn,ned->esd", up_grad, up_w, preferred_element_type=jnp.float32
    )
    hidden_all = hidden
    gate_all = gate_grad
    up_all = up_grad
    out_sum, in_grad, hidden_all, gate_all, up_all = (
        out_sum,
        in_grad,
        hidden_all,
        gate_all,
        up_all,
    )
    hidden_own, gate_own, up_own = (
        lax.all_to_all(hidden_all, "blk", split_axis=2, concat_axis=1, tiled=True),
        lax.all_to_all(gate_all, "blk", split_axis=2, concat_axis=1, tiled=True),
        lax.all_to_all(up_all, "blk", split_axis=2, concat_axis=1, tiled=True),
    )
    rows_in = lax.all_gather(expert_in, "blk", axis=1, tiled=True)
    rows_cot = lax.all_gather(expert_cot, "blk", axis=1, tiled=True)
    gate_w_grad = jnp.einsum("esn,esd->ned", gate_own, rows_in, preferred_element_type=jnp.float32)
    up_w_grad = jnp.einsum("esn,esd->ned", up_own, rows_in, preferred_element_type=jnp.float32)
    down_w_grad = jnp.einsum(
        "esn,esd->ned", hidden_own, rows_cot, preferred_element_type=jnp.float32
    )
    expert_grads = jnp.stack([gate_w_grad, up_w_grad, down_w_grad], axis=2)
    returned, returned_grad = (
        lax.all_to_all(
            out_sum.astype(jnp.bfloat16), "head", split_axis=1, concat_axis=0, tiled=True
        ),
        lax.all_to_all(
            in_grad.astype(jnp.bfloat16), "head", split_axis=1, concat_axis=0, tiled=True
        ),
    )
    outputs_pair = (
        jnp.concatenate([returned.reshape(-1, model_width), zero_row], axis=0)[target]
        .astype(jnp.float32)
        .reshape(tok_dev, 2, model_width)
    )
    input_pair = (
        jnp.concatenate([returned_grad.reshape(-1, model_width), zero_row], axis=0)[target]
        .astype(jnp.float32)
        .reshape(tok_dev, 2, model_width)
    )
    expert_input_grad = input_pair[:, 0] + input_pair[:, 1]
    branch, branch_back = jax.vjp(
        partial(branch_sum, choose=choose, live_rows=live_rows, real_count=real_count),
        router_prob,
        normed_two_f,
        const_w.astype(jnp.float32),
        vector_w.astype(jnp.float32),
        outputs_pair,
    )
    output = ((residual + branch) * live_rows[:, None]).astype(jnp.bfloat16)
    prob_grad, normed_grad_branch, const_grad, vector_grad, unused_grad = branch_back(out_grad)
    aux_grad = aux_weight * expert_count / live_total * fraction[None, :] * live_rows[:, None]
    normed_grad_router, router_grad, mixing_grad = router_back(prob_grad + aux_grad)
    normed_grad = normed_grad_router + normed_grad_branch + expert_input_grad
    residual_grad_norm, gain_two_grad = norm_two_back(normed_grad)
    residual_grad = out_grad + residual_grad_norm
    out_w_grad = jnp.dot(attended_tok.astype(jnp.float32).T, residual_grad, precision=highest)
    attended_grad = jnp.dot(residual_grad, out_w.astype(jnp.float32).T, precision=highest).astype(
        jnp.bfloat16
    )
    attended_grad_heads = lax.all_to_all(
        attended_grad, "head", split_axis=1, concat_axis=0, tiled=True
    )
    key_again, value_again = fetch_prev(key_heads, value_heads, span_count)
    query_grad, key_grad, value_grad = attend_backward(
        query_heads,
        key_again,
        value_again,
        attended_grad_heads,
        log_sums,
        blk_rows,
        key_ids,
        slot_size,
        lengths,
    )
    own_key = key_grad[:tok_blk]
    own_value = value_grad[:tok_blk]
    for offset in range(1, span_count):
        back_key, back_value = shifted(
            (
                for_sending(key_grad[offset * tok_blk : (offset + 1) * tok_blk]),
                for_sending(value_grad[offset * tok_blk : (offset + 1) * tok_blk]),
            ),
            "blk",
            -offset,
        )
        own_key = own_key + back_key
        own_value = own_value + back_value
    local_heads = query_heads.shape[1] // HD
    query_back = (
        rotary(query_grad.reshape(tok_blk, local_heads, HD), blk_pos, -1.0)
        .astype(jnp.bfloat16)
        .reshape(tok_blk, local_heads * HD)
    )
    key_back = (
        rotary(own_key.reshape(tok_blk, local_heads, HD), blk_pos, -1.0)
        .astype(jnp.bfloat16)
        .reshape(tok_blk, local_heads * HD)
    )
    value_back = own_value.astype(jnp.bfloat16)
    query_tok, key_tok, value_tok = (
        lax.all_to_all(query_back, "head", split_axis=0, concat_axis=1, tiled=True),
        lax.all_to_all(key_back, "head", split_axis=0, concat_axis=1, tiled=True),
        lax.all_to_all(value_back, "head", split_axis=0, concat_axis=1, tiled=True),
    )
    projected_grad = jnp.concatenate([query_tok, key_tok, value_tok], axis=1)
    qkv_grad = jnp.dot(normed_one_low.T, projected_grad, preferred_element_type=jnp.float32)
    normed_one_grad = jnp.dot(projected_grad, qkv_w.T, preferred_element_type=jnp.float32)
    inputs_grad_norm, gain_one_grad = norm_one_back(normed_one_grad)
    token_grad = (residual_grad + inputs_grad_norm).astype(jnp.bfloat16)
    weight_grads = (
        lax.psum_scatter(qkv_grad, ("head", "blk"), scatter_dimension=0, tiled=True),
        lax.psum_scatter(out_w_grad, ("head", "blk"), scatter_dimension=0, tiled=True),
        lax.psum_scatter(router_grad, ("head", "blk"), scatter_dimension=0, tiled=True),
        lax.psum_scatter(const_grad, ("head", "blk"), scatter_dimension=0, tiled=True),
        lax.psum_scatter(vector_grad, ("head", "blk"), scatter_dimension=0, tiled=True),
        lax.psum_scatter(
            jnp.stack([gain_one_grad, gain_two_grad], axis=1),
            ("head", "blk"),
            scatter_dimension=0,
            tiled=True,
        ),
    )
    mixing_total = lax.psum(mixing_grad, ("head", "blk"))
    return (
        output,
        aux_loss,
        token_grad,
        weight_grads[0],
        weight_grads[1],
        weight_grads[2],
        weight_grads[3],
        weight_grads[4],
        weight_grads[5],
        mixing_total,
        expert_grads,
    )


def solution(mesh):
    return jax.shard_map(
        on_device,
        mesh=mesh,
        in_specs=(
            P(("blk", "head"), None),
            P(("blk", "head"), None),
            P(("blk", "head"), None),
            P(("blk", "head"), None),
            P(),
            P(("head", "blk"), None),
            P(("head", "blk"), None),
            P(("head", "blk"), None),
            P(("head", "blk"), None),
            P(("head", "blk"), None),
            P(("head", "blk"), None),
            P(),
            P("blk", "head", None, None),
        ),
        out_specs=(
            P(("blk", "head"), None),
            P(),
            P(("blk", "head"), None),
            P(("head", "blk"), None),
            P(("head", "blk"), None),
            P(("head", "blk"), None),
            P(("head", "blk"), None),
            P(("head", "blk"), None),
            P(("head", "blk"), None),
            P(),
            P("blk", "head", None, None),
        ),
        check_vma=False,
    )
```

profile of v0, /device:TPU:0, one launch (start us, length us, event | category | flops | bytes accessed | tf_op | source)
XLA Modules:
  0.0 921.1 jit_solution(14666653857349578510)
XLA Ops:
  13.2 43.2 %all-gather = bf16[32,24,2]{1,2,0:T(2,128)(2,1)S(1)} all-gather(bf16[1,24,2]{1,2,0:T(2,128)(2,1)S(1)} %bitcast.453), channel_id=1, replica_groups=mesh['head'=2,'blk'=16] {'head','blk'}, dimensions={0}, use_global_device_ids=true | all-gather | bytes 3168 | tf_op jit(solution)/shard_map/all_gather | solution.py:210
  65.2 8.6 all-gather.10.cloned.1.call-done
  82.4 4.5 all-to-all-done
  91.0 4.1 all-to-all-done.1
  101.4 4.0 collective-permute-start.1
  105.4 3.7 collective-permute-start.2
  132.6 11.4 %collective-permute-start.10 = (bf16[256,384]{1,0:T(8,128)(2,1)S(1)}, bf16[256,384]{1,0:T(8,128)(2,1)S(1)}, u32[]{:S(2)}, u32[]{:S(2)}) collective-permute-start(bf16[256,384]{1,0:T(8,128)(2,1)S(1)} %bitcast.388), channel_id=1, source_target_pairs={{0,4},{1,5},{2,6},{3,7},{4,8},{5,9},{6,10},{7,11},{8,12},{9,13},{1... | collective-permute-start | bytes 589832 | tf_op jit(solution)/shard_map/ppermute | solution.py:23
  144.1 5.1 collective-permute-start.11
  150.6 17.1 %collective-permute-start.13 = (bf16[256,384]{1,0:T(8,128)(2,1)S(1)}, bf16[256,384]{1,0:T(8,128)(2,1)S(1)}, u32[]{:S(2)}, u32[]{:S(2)}) collective-permute-start(bf16[256,384]{1,0:T(8,128)(2,1)S(1)} %bitcast.391), channel_id=1, source_target_pairs={{0,7},{1,8},{2,9},{3,10},{4,11},{5,12},{6,13},{7,14},{8,15},{16,23... | collective-permute-start | bytes 589832 | tf_op jit(solution)/shard_map/ppermute | solution.py:23
  168.4 7.9 collective-permute-done.13
  176.9 61.8 %while.38 = (s32[]{:T(128)}, bf16[6,256,64]{1,2,0:T(8,128)(2,1)}, f32[6,256]{1,0:T(8,128)}, s32[1,2048]{1,0:T(1,128)}, s32[2048]{0:T(1024)S(1)}, /*index=5*/s32[...) while((s32[]{:T(128)}, bf16[6,256,64]{1,2,0:T(8,128)(2,1)}, ...), condition=%wide.region_5.6_spmd.clone.clone.clone, body=%wide.region_1.0_spmd.clone.clone.sunk.clone | while | flops 140591872 | bytes 7632623 | solution.py:94
  255.1 7.9 all_to_all.254
  264.4 75.9 %all-gather.3 = bf16[32,24,2]{1,2,0:T(2,128)(2,1)S(1)} all-gather(bf16[1,24,2]{1,2,0:T(2,128)(2,1)S(1)} %bitcast.454), channel_id=1, replica_groups=mesh['head'=2,'blk'=16] {'head','blk'}, dimensions={0}, use_global_device_ids=true | all-gather | bytes 3168 | tf_op jit(solution)/shard_map/all_gather | solution.py:209
  340.5 36.7 %all-gather.2 = bf16[32,24,4]{1,2,0:T(4,128)(2,1)S(1)} all-gather(bf16[1,24,4]{1,2,0:T(4,128)(2,1)S(1)} %bitcast.452), channel_id=1, replica_groups=mesh['head'=2,'blk'=16] {'head','blk'}, dimensions={0}, use_global_device_ids=true | all-gather | bytes 6336 | tf_op jit(solution)/shard_map/all_gather | solution.py:208
  377.3 39.0 %all-gather.1 = bf16[32,24,12]{1,2,0:T(8,128)(2,1)S(1)} all-gather(bf16[1,24,12]{1,2,0:T(8,128)(2,1)S(1)} %bitcast.444), channel_id=1, replica_groups=mesh['head'=2,'blk'=16] {'head','blk'}, dimensions={0}, use_global_device_ids=true | all-gather | bytes 19008 | tf_op jit(solution)/shard_map/all_gather | solution.py:207
  430.8 6.4 all-to-all-done.6
  439.2 6.8 fusion.58
  446.1 6.7 fusion.60
  452.9 9.6 %multiply_convert_fusion.1 = (bf16[4,48,2048]{2,1,0:T(8,128)(2,1)}, bf16[4,48,2048]{2,1,0:T(8,128)(2,1)}, bf16[4,48,2048]{2,1,0:T(8,128)(2,1)S(1)}) fusion(f32[4,48,2048]{2,1,0:T(8,128)S(1)} %fusion.58, f32[4,48,2048]{2,1,0:T(8,128)S(1)} %fusion.60, bf16[4,48,768]{2,1,0:T(8,128)(2,1)S(1)} %bitcast.372, ...), kind=kOutput, calls=%fused_computation.116 | convolution fusion | flops 609878016 | bytes 18382848 | tf_op jit(solution)/shard_map/esd,ned->esn/dot_general | solution.py:303
  462.5 7.0 fusion.66
  470.3 3.9 all-to-all-start.5
  474.2 7.1 fusion.57
  481.3 6.8 fusion.65
  489.0 4.1 all-to-all-start.7
  501.0 37.5 %psum.21 = f32[12]{0:T(128)S(1)} all-reduce(f32[12]{0:T(128)S(1)} %multiply_reduce_fusion.14), channel_id=1, replica_groups=mesh['head'=2,'blk'=16] {'head','blk'}, use_global_device_ids=true, to_apply=%region_21.22 | all-reduce | flops 12 | bytes 96 | tf_op jit(solution)/shard_map/psum | solution.py:262
  559.6 85.5 %while.39 = (s32[]{:T(128)}, f32[6,256,64]{1,2,0:T(8,128)}, f32[6,2048,64]{1,2,0:T(8,128)}, f32[6,2048,64]{1,2,0:T(8,128)}, s32[1,2048]{1,0:T(1,128)}, /*index=5...) while((s32[]{:T(128)}, f32[6,256,64]{1,2,0:T(8,128)}, ...), condition=%wide.region_42.43_spmd.clone.clone.clone, body=%wide.region_39.42_spmd.clone.clone.sunk.clone | while | flops 342590208 | bytes 31549708 | solution.py:132
  657.7 5.5 collective-permute-done.26
  670.3 13.3 %collective-permute-done.22 = bf16[256,384]{0,1:T(8,128)(2,1)S(1)} collective-permute-done((bf16[256,384]{0,1:T(8,128)(2,1)S(1)}, bf16[256,384]{0,1:T(8,128)(2,1)S(1)}, u32[]{:S(2)}, u32[]{:S(2)}) %collective-permute-start.22) | collective-permute-done | bytes 196640 | tf_op jit(solution)/shard_map/ppermute | solution.py:23
  693.4 10.0 %collective-permute-done.18 = bf16[256,384]{0,1:T(8,128)(2,1)S(1)} collective-permute-done((bf16[256,384]{0,1:T(8,128)(2,1)}, bf16[256,384]{0,1:T(8,128)(2,1)S(1)}, u32[]{:S(2)}, u32[]{:S(2)}) %collective-permute-start.18) | collective-permute-done | bytes 196640 | tf_op jit(solution)/shard_map/ppermute | solution.py:23
  703.5 9.4 %collective-permute-done.15 = bf16[256,384]{0,1:T(8,128)(2,1)S(1)} collective-permute-done((bf16[256,384]{0,1:T(8,128)(2,1)S(1)}, bf16[256,384]{0,1:T(8,128)(2,1)S(1)}, u32[]{:S(2)}, u32[]{:S(2)}) %collective-permute-start.15) | collective-permute-done | bytes 196640 | tf_op jit(solution)/shard_map/ppermute | solution.py:23
  719.3 4.0 all-to-all-done.10
  727.0 4.6 all-to-all-done.9
  731.6 4.1 fusion.107
  738.6 3.8 reshape.1259
  742.4 19.0 %all-to-all-start.14 = ((bf16[16,2,12288]{2,1,0:T(2,128)(2,1)}), bf16[16,2,12288]{2,1,0:T(2,128)(2,1)}, u32[]{:S(2)}, u32[]{:S(2)}) async-start(bf16[16,2,12288]{2,1,0:T(2,128)(2,1)} %reshape.1259), calls=%async_computation.16 | async-start | bytes 1572864 | tf_op jit(solution)/shard_map/all_to_all | solution.py:323
  764.4 3.8 reshape.1261
  768.2 11.9 %all-to-all-done.14 = bf16[16,2,12288]{2,1,0:T(2,128)(2,1)} async-done(((bf16[16,2,12288]{2,1,0:T(2,128)(2,1)}), bf16[16,2,12288]{2,1,0:T(2,128)(2,1)}, u32[]{:S(2)}, u32[]{:S(2)}) %all-to-all-start.14) | async-done | bytes 786464 | tf_op jit(solution)/shard_map/all_to_all | solution.py:323
  780.2 5.5 all-to-all-start.13
  788.9 3.9 reshape.1263
  793.1 11.5 %all-to-all-done.13 = bf16[16,2,12288]{2,1,0:T(2,128)(2,1)} async-done(((bf16[16,2,12288]{2,1,0:T(2,128)(2,1)}), bf16[16,2,12288]{2,1,0:T(2,128)(2,1)}, u32[]{:S(2)}, u32[]{:S(2)}) %all-to-all-start.13) | async-done | bytes 786464 | tf_op jit(solution)/shard_map/all_to_all | solution.py:325
  804.6 13.2 %all-to-all-start.12 = ((bf16[16,2,12288]{2,1,0:T(2,128)(2,1)}), bf16[16,2,12288]{2,1,0:T(2,128)(2,1)}, u32[]{:S(2)}, u32[]{:S(2)}) async-start(bf16[16,2,12288]{2,1,0:T(2,128)(2,1)} %reshape.1263), calls=%async_computation.14 | async-start | bytes 1572864 | tf_op jit(solution)/shard_map/all_to_all | solution.py:324
  821.5 43.2 %all-reduce.17 = (f32[12]{0:T(128)S(1)}, f32[768,12]{0,1:T(8,128)S(1)}, f32[768,4]{0,1:T(4,128)S(1)}, f32[768,2]{0,1:T(2,128)S(1)}, f32[768,2]{0,1:T(2,128)S(1)}, /*index=5*/f32[12,12]{0,1:T(8,128)S(1)}) all-reduce(f32[12]{0:T(128)S(1)} %copy-done.75, f32[768,12]{0,1:T(8,128)S(1)} %fusion.148, ...), channel_id=1, replica_groups=mesh['head'=2,'blk'=16] {'head','blk'}, use_global_device_ids=true, to_apply=%region_24.25 | all-reduce | flops 15516 | bytes 124128 | tf_op jit(solution)/shard_map/psum | solution.py:262
  870.0 5.6 reshape.1260
  877.9 5.6 reshape.1262
  884.9 5.6 reshape.1264
  893.1 4.2 convolution_bitcast_fusion.3
  899.2 4.3 convolution_bitcast_fusion.2
  906.0 6.6 copy.298
  (763 shorter events, 317.5 us)
Async XLA Ops:
  7.2 66.6 %all-gather.10.cloned.1.call-start = ((), (), s32[]{:S(2)}) async-start(), calls=%async_computation.17 | async-start | bytes 3649536 | tf_op jit(solution)/shard_map/all_gather | solution.py:205
  7.9 239.1 %all-gather.12.cloned.1.call-start = ((), (), s32[]{:S(2)}) async-start(), calls=%async_computation.18 | async-start | bytes 1216512 | tf_op jit(solution)/shard_map/all_gather | solution.py:206
  8.7 430.6 %all-gather.14.cloned.1.call-start = ((), (), s32[]{:S(2)}) async-start(), calls=%async_computation.19 | async-start | bytes 40108032 | tf_op jit(solution)/shard_map/all_gather | solution.py:293
  78.2 8.6 all-to-all-start
  86.9 8.2 all-to-all-start.1
  95.1 18.8 %all-to-all-start.2 = ((bf16[128,2,384]{0,2,1:T(8,128)(2,1)}), bf16[128,2,384]{0,2,1:T(8,128)(2,1)S(1)}, u32[]{:S(2)}, u32[]{:S(2)}) async-start(bf16[128,2,384]{0,2,1:T(8,128)(2,1)} %bitcast.26), calls=%async_computation.2 | async-start | bytes 393216 | tf_op jit(solution)/shard_map/all_to_all | solution.py:233
  99.4 17.3 %collective-permute-start = (bf16[256,384]{1,0:T(8,128)(2,1)}, bf16[256,384]{1,0:T(8,128)(2,1)}, u32[]{:S(2)}, u32[]{:S(2)}) collective-permute-start(bf16[256,384]{1,0:T(8,128)(2,1)} %bitcast.25), channel_id=1, source_target_pairs={{0,1},{1,2},{2,3},{3,4},{4,5},{5,6},{6,7},{7,8},{8,9},{9,10},{10,1... | collective-permute-start | bytes 589832 | tf_op jit(solution)/shard_map/ppermute | solution.py:23
  101.4 18.8 %collective-permute-start.1 = (bf16[256,384]{1,0:T(8,128)(2,1)}, bf16[256,384]{1,0:T(8,128)(2,1)}, u32[]{:S(2)}, u32[]{:S(2)}) collective-permute-start(bf16[256,384]{1,0:T(8,128)(2,1)} %bitcast.25), channel_id=1, source_target_pairs={{0,2},{1,3},{2,4},{3,5},{4,6},{5,7},{6,8},{7,9},{8,10},{9,11},{10,... | collective-permute-start | bytes 589832 | tf_op jit(solution)/shard_map/ppermute | solution.py:23
  105.4 17.1 %collective-permute-start.2 = (bf16[256,384]{1,0:T(8,128)(2,1)}, bf16[256,384]{1,0:T(8,128)(2,1)}, u32[]{:S(2)}, u32[]{:S(2)}) collective-permute-start(bf16[256,384]{1,0:T(8,128)(2,1)} %bitcast.25), channel_id=1, source_target_pairs={{0,3},{1,4},{2,5},{3,6},{4,7},{5,8},{6,9},{7,10},{8,11},{9,12},{10... | collective-permute-start | bytes 589832 | tf_op jit(solution)/shard_map/ppermute | solution.py:23
  109.1 16.7 %collective-permute-start.3 = (bf16[256,384]{1,0:T(8,128)(2,1)}, bf16[256,384]{1,0:T(8,128)(2,1)}, u32[]{:S(2)}, u32[]{:S(2)}) collective-permute-start(bf16[256,384]{1,0:T(8,128)(2,1)} %bitcast.25), channel_id=1, source_target_pairs={{0,4},{1,5},{2,6},{3,7},{4,8},{5,9},{6,10},{7,11},{8,12},{9,13},{1... | collective-permute-start | bytes 589832 | tf_op jit(solution)/shard_map/ppermute | solution.py:23
  111.8 17.8 %collective-permute-start.4 = (bf16[256,384]{1,0:T(8,128)(2,1)}, bf16[256,384]{1,0:T(8,128)(2,1)}, u32[]{:S(2)}, u32[]{:S(2)}) collective-permute-start(bf16[256,384]{1,0:T(8,128)(2,1)} %bitcast.25), channel_id=1, source_target_pairs={{0,5},{1,6},{2,7},{3,8},{4,9},{5,10},{6,11},{7,12},{8,13},{9,14},{... | collective-permute-start | bytes 589832 | tf_op jit(solution)/shard_map/ppermute | solution.py:23
  116.7 15.9 %collective-permute-start.5 = (bf16[256,384]{1,0:T(8,128)(2,1)}, bf16[256,384]{1,0:T(8,128)(2,1)S(1)}, u32[]{:S(2)}, u32[]{:S(2)}) collective-permute-start(bf16[256,384]{1,0:T(8,128)(2,1)} %bitcast.25), channel_id=1, source_target_pairs={{0,6},{1,7},{2,8},{3,9},{4,10},{5,11},{6,12},{7,13},{8,14},{9,15},... | collective-permute-start | bytes 589832 | tf_op jit(solution)/shard_map/ppermute | solution.py:23
  120.2 23.9 %collective-permute-start.6 = (bf16[256,384]{1,0:T(8,128)(2,1)}, bf16[256,384]{1,0:T(8,128)(2,1)S(1)}, u32[]{:S(2)}, u32[]{:S(2)}) collective-permute-start(bf16[256,384]{1,0:T(8,128)(2,1)} %bitcast.25), channel_id=1, source_target_pairs={{0,7},{1,8},{2,9},{3,10},{4,11},{5,12},{6,13},{7,14},{8,15},{16,23... | collective-permute-start | bytes 589832 | tf_op jit(solution)/shard_map/ppermute | solution.py:23
  122.5 26.7 %collective-permute-start.7 = (bf16[256,384]{1,0:T(8,128)(2,1)}, bf16[256,384]{1,0:T(8,128)(2,1)S(1)}, u32[]{:S(2)}, u32[]{:S(2)}) collective-permute-start(bf16[256,384]{1,0:T(8,128)(2,1)} %bitcast.385), channel_id=1, source_target_pairs={{0,1},{1,2},{2,3},{3,4},{4,5},{5,6},{6,7},{7,8},{8,9},{9,10},{10,1... | collective-permute-start | bytes 589832 | tf_op jit(solution)/shard_map/ppermute | solution.py:23
  125.8 24.8 %collective-permute-start.8 = (bf16[256,384]{1,0:T(8,128)(2,1)}, bf16[256,384]{1,0:T(8,128)(2,1)S(1)}, u32[]{:S(2)}, u32[]{:S(2)}) collective-permute-start(bf16[256,384]{1,0:T(8,128)(2,1)} %bitcast.386), channel_id=1, source_target_pairs={{0,2},{1,3},{2,4},{3,5},{4,6},{5,7},{6,8},{7,9},{8,10},{9,11},{10,... | collective-permute-start | bytes 589832 | tf_op jit(solution)/shard_map/ppermute | solution.py:23
  129.6 38.2 %collective-permute-start.9 = (bf16[256,384]{1,0:T(8,128)(2,1)S(1)}, bf16[256,384]{1,0:T(8,128)(2,1)S(1)}, u32[]{:S(2)}, u32[]{:S(2)}) collective-permute-start(bf16[256,384]{1,0:T(8,128)(2,1)S(1)} %bitcast.387), channel_id=1, source_target_pairs={{0,3},{1,4},{2,5},{3,6},{4,7},{5,8},{6,9},{7,10},{8,11},{9,12},{10... | collective-permute-start | bytes 589832 | tf_op jit(solution)/shard_map/ppermute | solution.py:23
  132.6 35.2 %collective-permute-start.10 = (bf16[256,384]{1,0:T(8,128)(2,1)S(1)}, bf16[256,384]{1,0:T(8,128)(2,1)S(1)}, u32[]{:S(2)}, u32[]{:S(2)}) collective-permute-start(bf16[256,384]{1,0:T(8,128)(2,1)S(1)} %bitcast.388), channel_id=1, source_target_pairs={{0,4},{1,5},{2,6},{3,7},{4,8},{5,9},{6,10},{7,11},{8,12},{9,13},{1... | collective-permute-start | bytes 589832 | tf_op jit(solution)/shard_map/ppermute | solution.py:23
  144.1 23.8 %collective-permute-start.11 = (bf16[256,384]{1,0:T(8,128)(2,1)S(1)}, bf16[256,384]{1,0:T(8,128)(2,1)S(1)}, u32[]{:S(2)}, u32[]{:S(2)}) collective-permute-start(bf16[256,384]{1,0:T(8,128)(2,1)S(1)} %bitcast.389), channel_id=1, source_target_pairs={{0,5},{1,6},{2,7},{3,8},{4,9},{5,10},{6,11},{7,12},{8,13},{9,14},{... | collective-permute-start | bytes 589832 | tf_op jit(solution)/shard_map/ppermute | solution.py:23
  149.2 19.2 %collective-permute-start.12 = (bf16[256,384]{1,0:T(8,128)(2,1)S(1)}, bf16[256,384]{1,0:T(8,128)(2,1)S(1)}, u32[]{:S(2)}, u32[]{:S(2)}) collective-permute-start(bf16[256,384]{1,0:T(8,128)(2,1)S(1)} %bitcast.390), channel_id=1, source_target_pairs={{0,6},{1,7},{2,8},{3,9},{4,10},{5,11},{6,12},{7,13},{8,14},{9,15},... | collective-permute-start | bytes 589832 | tf_op jit(solution)/shard_map/ppermute | solution.py:23
  150.6 25.8 %collective-permute-start.13 = (bf16[256,384]{1,0:T(8,128)(2,1)S(1)}, bf16[256,384]{1,0:T(8,128)(2,1)S(1)}, u32[]{:S(2)}, u32[]{:S(2)}) collective-permute-start(bf16[256,384]{1,0:T(8,128)(2,1)S(1)} %bitcast.391), channel_id=1, source_target_pairs={{0,7},{1,8},{2,9},{3,10},{4,11},{5,12},{6,13},{7,14},{8,15},{16,23... | collective-permute-start | bytes 589832 | tf_op jit(solution)/shard_map/ppermute | solution.py:23
  242.2 8.3 all-to-all-start.3
  245.7 647.4 %all-gather.16.cloned.1.call-start = ((), (), s32[]{:S(2)}) async-start(), calls=%async_computation.22 | async-start | bytes 5013504 | tf_op jit(solution)/shard_map/all_gather | solution.py:327
  427.2 9.9 %all-to-all-start.6 = ((bf16[8,24,768]{2,1,0:T(8,128)(2,1)}), bf16[8,24,768]{2,1,0:T(8,128)(2,1)S(1)}, u32[]{:S(2)}, u32[]{:S(2)}) async-start(bf16[8,24,768]{2,1,0:T(8,128)(2,1)} %bitcast.369), calls=%async_computation.6 | async-start | bytes 589824 | tf_op jit(solution)/shard_map/all_to_all | solution.py:291
  430.7 468.5 %all-gather.18.cloned.1.call-start = ((), (), s32[]{:S(2)}) async-start(), calls=%async_computation.23 | async-start | bytes 5013504 | tf_op jit(solution)/shard_map/all_gather | solution.py:328
  470.3 18.7 %all-to-all-start.5 = ((bf16[4,48,768]{2,0,1:T(4,128)(2,1)}), bf16[4,48,768]{2,0,1:T(4,128)(2,1)S(1)}, u32[]{:S(2)}, u32[]{:S(2)}) async-start(bf16[4,48,768]{2,0,1:T(4,128)(2,1)} %copy.274), calls=%async_computation.5 | async-start | bytes 589824 | tf_op jit(solution)/shard_map/all_to_all | solution.py:336
  489.0 49.6 %all-to-all-start.7 = ((bf16[4,48,768]{2,0,1:T(4,128)(2,1)}), bf16[4,48,768]{2,0,1:T(4,128)(2,1)}, u32[]{:S(2)}, u32[]{:S(2)}) async-start(bf16[4,48,768]{2,0,1:T(4,128)(2,1)} %copy.282), calls=%async_computation.7 | async-start | bytes 589824 | tf_op jit(solution)/shard_map/all_to_all | solution.py:339
  551.1 8.5 all-to-all-start.8
  554.6 358.0 %reduce-scatter.9.cloned.1.call-start = ((), (), s32[]{:S(2)}) async-start(), calls=%async_computation.21 | async-start | bytes 2433024 | tf_op jit(solution)/shard_map/reduce_scatter | solution.py:425
  647.6 8.8 collective-permute-start.27
  648.9 14.3 %collective-permute-start.26 = (bf16[256,384]{0,1:T(8,128)(2,1)S(1)}, bf16[256,384]{0,1:T(8,128)(2,1)S(1)}, u32[]{:S(2)}, u32[]{:S(2)}) collective-permute-start(bf16[256,384]{0,1:T(8,128)(2,1)S(1)} %bitcast.412), channel_id=1, source_target_pairs={{6,0},{7,1},{8,2},{9,3},{10,4},{11,5},{12,6},{13,7},{14,8},{15,9},... | collective-permute-start | bytes 589832 | tf_op jit(solution)/shard_map/ppermute | solution.py:23
  650.2 14.2 %collective-permute-start.25 = (bf16[256,384]{0,1:T(8,128)(2,1)S(1)}, bf16[256,384]{0,1:T(8,128)(2,1)S(1)}, u32[]{:S(2)}, u32[]{:S(2)}) collective-permute-start(bf16[256,384]{0,1:T(8,128)(2,1)S(1)} %bitcast.411), channel_id=1, source_target_pairs={{5,0},{6,1},{7,2},{8,3},{9,4},{10,5},{11,6},{12,7},{13,8},{14,9},{... | collective-permute-start | bytes 589832 | tf_op jit(solution)/shard_map/ppermute | solution.py:23
  651.5 14.3 %collective-permute-start.24 = (bf16[256,384]{0,1:T(8,128)(2,1)S(1)}, bf16[256,384]{0,1:T(8,128)(2,1)S(1)}, u32[]{:S(2)}, u32[]{:S(2)}) collective-permute-start(bf16[256,384]{0,1:T(8,128)(2,1)S(1)} %bitcast.410), channel_id=1, source_target_pairs={{4,0},{5,1},{6,2},{7,3},{8,4},{9,5},{10,6},{11,7},{12,8},{13,9},{1... | collective-permute-start | bytes 589832 | tf_op jit(solution)/shard_map/ppermute | solution.py:23
  652.8 16.2 %collective-permute-start.23 = (bf16[256,384]{0,1:T(8,128)(2,1)S(1)}, bf16[256,384]{0,1:T(8,128)(2,1)S(1)}, u32[]{:S(2)}, u32[]{:S(2)}) collective-permute-start(bf16[256,384]{0,1:T(8,128)(2,1)S(1)} %bitcast.408), channel_id=1, source_target_pairs={{3,0},{4,1},{5,2},{6,3},{7,4},{8,5},{9,6},{10,7},{11,8},{12,9},{13... | collective-permute-start | bytes 589832 | tf_op jit(solution)/shard_map/ppermute | solution.py:23
  656.4 27.2 %collective-permute-start.22 = (bf16[256,384]{0,1:T(8,128)(2,1)S(1)}, bf16[256,384]{0,1:T(8,128)(2,1)S(1)}, u32[]{:S(2)}, u32[]{:S(2)}) collective-permute-start(bf16[256,384]{0,1:T(8,128)(2,1)S(1)} %bitcast.406), channel_id=1, source_target_pairs={{2,0},{3,1},{4,2},{5,3},{6,4},{7,5},{8,6},{9,7},{10,8},{11,9},{12,... | collective-permute-start | bytes 589832 | tf_op jit(solution)/shard_map/ppermute | solution.py:23
  663.1 21.7 %collective-permute-start.21 = (bf16[256,384]{0,1:T(8,128)(2,1)S(1)}, bf16[256,384]{0,1:T(8,128)(2,1)S(1)}, u32[]{:S(2)}, u32[]{:S(2)}) collective-permute-start(bf16[256,384]{0,1:T(8,128)(2,1)S(1)} %bitcast.405), channel_id=1, source_target_pairs={{1,0},{2,1},{3,2},{4,3},{5,4},{6,5},{7,6},{8,7},{9,8},{10,9},{11,1... | collective-permute-start | bytes 589832 | tf_op jit(solution)/shard_map/ppermute | solution.py:23
  664.4 21.7 %collective-permute-start.20 = (bf16[256,384]{0,1:T(8,128)(2,1)S(1)}, bf16[256,384]{0,1:T(8,128)(2,1)S(1)}, u32[]{:S(2)}, u32[]{:S(2)}) collective-permute-start(bf16[256,384]{0,1:T(8,128)(2,1)S(1)} %bitcast.409), channel_id=1, source_target_pairs={{7,0},{8,1},{9,2},{10,3},{11,4},{12,5},{13,6},{14,7},{15,8},{23,16... | collective-permute-start | bytes 589832 | tf_op jit(solution)/shard_map/ppermute | solution.py:23
  665.8 21.7 %collective-permute-start.19 = (bf16[256,384]{0,1:T(8,128)(2,1)S(1)}, bf16[256,384]{0,1:T(8,128)(2,1)S(1)}, u32[]{:S(2)}, u32[]{:S(2)}) collective-permute-start(bf16[256,384]{0,1:T(8,128)(2,1)S(1)} %bitcast.407), channel_id=1, source_target_pairs={{6,0},{7,1},{8,2},{9,3},{10,4},{11,5},{12,6},{13,7},{14,8},{15,9},... | collective-permute-start | bytes 589832 | tf_op jit(solution)/shard_map/ppermute | solution.py:23
  669.0 34.5 %collective-permute-start.18 = (bf16[256,384]{0,1:T(8,128)(2,1)}, bf16[256,384]{0,1:T(8,128)(2,1)S(1)}, u32[]{:S(2)}, u32[]{:S(2)}) collective-permute-start(bf16[256,384]{0,1:T(8,128)(2,1)} %bitcast.84), channel_id=1, source_target_pairs={{5,0},{6,1},{7,2},{8,3},{9,4},{10,5},{11,6},{12,7},{13,8},{14,9},{... | collective-permute-start | bytes 589832 | tf_op jit(solution)/shard_map/ppermute | solution.py:23
  683.6 19.9 %collective-permute-start.17 = (bf16[256,384]{0,1:T(8,128)(2,1)}, bf16[256,384]{0,1:T(8,128)(2,1)S(1)}, u32[]{:S(2)}, u32[]{:S(2)}) collective-permute-start(bf16[256,384]{0,1:T(8,128)(2,1)} %bitcast.83), channel_id=1, source_target_pairs={{4,0},{5,1},{6,2},{7,3},{8,4},{9,5},{10,6},{11,7},{12,8},{13,9},{1... | collective-permute-start | bytes 589832 | tf_op jit(solution)/shard_map/ppermute | solution.py:23
  684.9 18.6 %collective-permute-start.16 = (bf16[256,384]{0,1:T(8,128)(2,1)}, bf16[256,384]{0,1:T(8,128)(2,1)S(1)}, u32[]{:S(2)}, u32[]{:S(2)}) collective-permute-start(bf16[256,384]{0,1:T(8,128)(2,1)} %bitcast.82), channel_id=1, source_target_pairs={{3,0},{4,1},{5,2},{6,3},{7,4},{8,5},{9,6},{10,7},{11,8},{12,9},{13... | collective-permute-start | bytes 589832 | tf_op jit(solution)/shard_map/ppermute | solution.py:23
  686.2 26.7 %collective-permute-start.15 = (bf16[256,384]{0,1:T(8,128)(2,1)S(1)}, bf16[256,384]{0,1:T(8,128)(2,1)S(1)}, u32[]{:S(2)}, u32[]{:S(2)}) collective-permute-start(bf16[256,384]{0,1:T(8,128)(2,1)S(1)} %bitcast.404), channel_id=1, source_target_pairs={{2,0},{3,1},{4,2},{5,3},{6,4},{7,5},{8,6},{9,7},{10,8},{11,9},{12,... | collective-permute-start | bytes 589832 | tf_op jit(solution)/shard_map/ppermute | solution.py:23
  687.5 26.4 %collective-permute-start.14 = (bf16[256,384]{0,1:T(8,128)(2,1)S(1)}, bf16[256,384]{0,1:T(8,128)(2,1)S(1)}, u32[]{:S(2)}, u32[]{:S(2)}) collective-permute-start(bf16[256,384]{0,1:T(8,128)(2,1)S(1)} %bitcast.403), channel_id=1, source_target_pairs={{1,0},{2,1},{3,2},{4,3},{5,4},{6,5},{7,6},{8,7},{9,8},{10,9},{11,1... | collective-permute-start | bytes 589832 | tf_op jit(solution)/shard_map/ppermute | solution.py:23
  690.0 25.1 %all-to-all-start.11 = ((bf16[2,128,384]{2,1,0:T(8,128)(2,1)}), bf16[2,128,384]{2,1,0:T(8,128)(2,1)S(1)}, u32[]{:S(2)}, u32[]{:S(2)}) async-start(bf16[2,128,384]{2,1,0:T(8,128)(2,1)} %bitcast.99), calls=%async_computation.11 | async-start | bytes 393216 | tf_op jit(solution)/shard_map/all_to_all | solution.py:416
  715.1 8.2 all-to-all-start.10
  726.8 185.9 %reduce-scatter.7.cloned.1.call-start = ((), (), s32[]{:S(2)}) async-start(), calls=%async_computation.20 | async-start | bytes 7299072 | tf_op jit(solution)/shard_map/reduce_scatter | solution.py:424
  742.4 37.8 %all-to-all-start.14 = ((bf16[16,2,12288]{2,1,0:T(2,128)(2,1)}), bf16[16,2,12288]{2,1,0:T(2,128)(2,1)}, u32[]{:S(2)}, u32[]{:S(2)}) async-start(bf16[16,2,12288]{2,1,0:T(2,128)(2,1)} %reshape.1259), calls=%async_computation.16 | async-start | bytes 1572864 | tf_op jit(solution)/shard_map/all_to_all | solution.py:323
  780.2 24.4 %all-to-all-start.13 = ((bf16[16,2,12288]{2,1,0:T(2,128)(2,1)}), bf16[16,2,12288]{2,1,0:T(2,128)(2,1)}, u32[]{:S(2)}, u32[]{:S(2)}) async-start(bf16[16,2,12288]{2,1,0:T(2,128)(2,1)} %reshape.1261), calls=%async_computation.15 | async-start | bytes 1572864 | tf_op jit(solution)/shard_map/all_to_all | solution.py:325
  804.6 80.3 %all-to-all-start.12 = ((bf16[16,2,12288]{2,1,0:T(2,128)(2,1)}), bf16[16,2,12288]{2,1,0:T(2,128)(2,1)}, u32[]{:S(2)}, u32[]{:S(2)}) async-start(bf16[16,2,12288]{2,1,0:T(2,128)(2,1)} %reshape.1263), calls=%async_computation.14 | async-start | bytes 1572864 | tf_op jit(solution)/shard_map/all_to_all | solution.py:324
  (135 other events, 2627.8 us)
Sparse Core Ops, SparseCore 0:
  10.9 62.8 all-gather.9
  76.7 53.0 all-gather.11
  131.3 205.5 all-gather.13
  339.1 80.4 all-gather.15
  438.0 49.6 all-gather.17
  561.0 105.9 reduce-scatter.8
  735.8 145.4 reduce-scatter.6
where the time goes:
time: 935 us; the launch traced here: 921 us
  blocking collectives  283 us (30%)
  starting transfers between devices  156 us (17%)
  matrix products  148 us (16%)
  local copies, waits for them, and re-layouts  126 us (13%)
  waiting for transfers between devices  112 us (12%)
  other arithmetic  57.5 us (6%)
  loops' own time  20.5 us (2%)
  between operations  19.4 us (2%)
    psum x2, blocking collectives, on_device(): count_all, prob_all = lax.psum((count_local, prob_local), ('head', 'blk'))  80.7 us
    ppermute x28, starting transfers between devices, shifted(): return lax.ppermute(block, axis, route)  78.5 us
    all_gather x1, blocking collectives, on_device(): lax.all_gather(const_vec, ('head', 'blk'), axis=0, tiled=True)  75.9 us
    unnamed x204, local copies, waits for them, and re-layouts  50.7 us
    ppermute x28, waiting for transfers between devices, shifted(): return lax.ppermute(block, axis, route)  48.8 us
    all_gather x1, blocking collectives, on_device(): lax.all_gather(norm_gains, ('head', 'blk'), axis=0, tiled=True)  43.2 us
    all_gather x1, blocking collectives, on_device(): lax.all_gather(w_router, ('head', 'blk'), axis=0, tiled=True)  39 us
    all_gather x1, blocking collectives, on_device(): lax.all_gather(w_const, ('head', 'blk'), axis=0, tiled=True)  36.7 us
  transfers between devices with their start and end apart: 49, of which 18 were waited for; matrix products, arithmetic and copies ran while one was open for 36% of the time, Pallas kernels for 0%

commit v1 on v0

--- a/solution.py
+++ b/solution.py
@@ -1,13 +1,565 @@
 from functools import partial
+import functools
 import math
 
 import jax
 import jax.numpy as jnp
+import numpy as np
 from jax import lax
+from jax.experimental import pallas as pl
+from jax.experimental.pallas import tpu as pltpu
 from jax.sharding import PartitionSpec as P
 
 HEADS = 12
+MESH = pl.DeviceIdType.MESH
+f32, bf16 = jnp.float32, jnp.bfloat16
+NEG = -1e30
 HD = 64
+X, C, Y, Z = 1, 2, 4, 8
+
+
+def place(mask, h, b):
+    hb = 1 - h if mask & X else h
+    cb = b % 2
+    yb = (b // 2) % 2
+    zb = (b // 4) % 2
+    cb = 1 - cb if mask & C else cb
+    yb = 1 - yb if mask & Y else yb
+    zb = 1 - zb if mask & Z else zb
+    low = zb * 4 + yb * 2 + cb
+    return hb, (b // 8) * 8 + low, low * 2 + hb
+
+
+def head_of(h, b):
+    quad = b % 4
+    return h * 6 + ((b % 8) // 4) * 3 + quad - quad // 3
+
+
+def home_of(head):
+    h, i = head // 6, head % 6
+    return ((i // 3) * 4 + i % 3) * 2 + h
+
+
+def greet(masks_or_all, h, b, n_blk):
+    barrier = pltpu.get_barrier_semaphore()
+    if masks_or_all == "all":
+        me = b * 2 + h
+        total = 2 * n_blk
+
+        def say(k, carry):
+            other = (me + k) % total
+            pl.semaphore_signal(barrier, inc=1, device_id=(other % 2, other // 2), device_id_type=MESH)
+            return carry
+
+        lax.fori_loop(1, total, say, 0)
+        pl.semaphore_wait(barrier, total - 1)
+    else:
+        for m in masks_or_all:
+            ph, pb, _ = place(m, h, b)
+            pl.semaphore_signal(barrier, inc=1, device_id=(ph, pb), device_id_type=MESH)
+        pl.semaphore_wait(barrier, len(masks_or_all))
+
+
+def turned(qk, cos, sin):
+    lane = lax.broadcasted_iota(jnp.int32, qk.shape, 1)
+    swapped = jnp.where(lane % 64 < 32, pltpu.roll(qk, 96, 1), pltpu.roll(qk, 32, 1))
+    return qk * cos + swapped * sin
+
+
+def rotary_tables(rows):
+    freq = np.exp(np.arange(32, dtype=np.float32) * np.float32(-2.0 * math.log(10000.0) / 64)).astype(np.float32)
+    ang = (np.arange(rows, dtype=np.float32)[:, None] * freq[None, :]).astype(np.float32).astype(np.float64)
+    cos, sin = np.cos(ang), np.sin(ang)
+    return (
+        np.concatenate([cos, cos, cos, cos], 1).astype(np.float32),
+        np.concatenate([-sin, sin, -sin, sin], 1).astype(np.float32),
+    )
+
+
+def forward_kernel(
+    n_blk, lengths, tok, w_in, small_in, cos_hbm, sin_hbm,
+    norm_hbm, q_hbm, k_hbm, v_hbm, o_hbm, att_out, sm_out, smt_out,
+    xg, pieces, got, w_f, w_b, cos, sin, norm, q, k, v, o, sendbuf, att_in,
+    ag_send, ag_recv, pc_send, pc_recv, at_send, at_recv, loc,
+):
+    h, b = lax.axis_index("head"), lax.axis_index("blk")
+    me = b * 2 + h
+    total = 2 * n_blk
+    _, _, rank = place(0, h, b)
+    cos_in = pltpu.make_async_copy(cos_hbm, cos, loc.at[0])
+    sin_in = pltpu.make_async_copy(sin_hbm, sin, loc.at[1])
+    cos_in.start()
+    sin_in.start()
+    for p in range(3):
+        xg[p, rank] = tok[:, 256 * p : 256 * p + 256]
+    greet("all", h, b, n_blk)
+
+    def block_copy(p, m, d, slot):
+        _, _, r = place(m, h, b)
+        ph, pb, _ = place(d, h, b)
+        return pltpu.make_async_remote_copy(
+            src_ref=xg.at[p, r], dst_ref=xg.at[p, r],
+            send_sem=ag_send.at[p, slot], recv_sem=ag_recv.at[p, m ^ d],
+            device_id=(ph, pb), device_id_type=MESH,
+        )
+
+    def arrival(p, m):
+        _, _, r = place(m, h, b)
+        return pltpu.make_async_remote_copy(
+            src_ref=xg.at[p, r], dst_ref=xg.at[p, r],
+            send_sem=ag_send.at[p, 0], recv_sem=ag_recv.at[p, m],
+            device_id=(h, b), device_id_type=MESH,
+        )
+
+    sends = []
+    counts = [0, 0, 0]
+
+    def send(p, m, d):
+        copy = block_copy(p, m, d, counts[p])
+        counts[p] += 1
+        copy.start()
+        sends.append(copy)
+
+    dims = [X, Y, Z]
+    orders = [dims[p:] + dims[:p] for p in range(3)]
+    for t in range(3):
+        for p in range(3):
+            send(p, 0, orders[p][t])
+    for p in range(3):
+        send(p, 0, C)
+
+    w24 = w_in[...].astype(f32)
+    small = small_in[...]
+    for j in range(12):
+        cat = jnp.concatenate(
+            [w24[:, 64 * j : 64 * j + 64], w24[:, 768 + 64 * j : 832 + 64 * j],
+             w24[:, 1536 + 64 * j : 1600 + 64 * j], small], axis=1)
+        pieces[j, :, 0:256] = cat[0:16].astype(bf16)
+        pieces[j, :, 256:384] = jnp.concatenate([cat[16:24, 0:128], cat[16:24, 128:256]], axis=0).astype(bf16)
+
+    def piece_copy(kk):
+        other = (me + kk) % total
+        oh, ob = other % 2, other // 2
+        return pltpu.make_async_remote_copy(
+            src_ref=pieces.at[head_of(oh, ob)], dst_ref=got.at[me],
+            send_sem=pc_send.at[kk], recv_sem=pc_recv.at[me],
+            device_id=(oh, ob), device_id_type=MESH,
+        )
+
+    def send_piece(kk, carry):
+        piece_copy(kk).start()
+        return carry
+
+    lax.fori_loop(1, total, send_piece, 0)
+    got[me] = pieces[head_of(h, b)]
+
+    for p in range(3):
+        d0, d1, d2 = orders[p]
+        arrival(p, d0).wait_recv()
+        for d in (d1, d2, C):
+            send(p, d0, d)
+    for p in range(3):
+        d0, d1, d2 = orders[p]
+        for m in (d1, d0 ^ d1):
+            arrival(p, m).wait_recv()
+            for d in (d2, C):
+                send(p, m, d)
+    for p in range(3):
+        d0, d1, d2 = orders[p]
+        for m in (d2, d0 ^ d2, d1 ^ d2, d0 ^ d1 ^ d2):
+            arrival(p, m).wait_recv()
+            send(p, m, C)
+
+    def take_piece(kk, carry):
+        src = (me + kk) % total
+        pltpu.make_async_remote_copy(
+            src_ref=pieces.at[0], dst_ref=got.at[src],
+            send_sem=pc_send.at[0], recv_sem=pc_recv.at[src],
+            device_id=(h, b), device_id_type=MESH,
+        ).wait_recv()
+        return carry
+
+    lax.fori_loop(1, total, take_piece, 0)
+
+    for src in range(2 * n_blk):
+        row = 24 * ((src % 2) * n_blk + src // 2)
+        w_f[row : row + 16, :] = got[src, :, 0:256].astype(f32)
+        low = got[src, :, 256:384].astype(f32)
+        w_f[row + 16 : row + 24, 0:128] = low[0:8]
+        w_f[row + 16 : row + 24, 128:256] = low[8:16]
+    w_b[...] = w_f[...].astype(bf16)
+    sm_out[...] = w_f[:, 128:256]
+    smt = jnp.transpose(w_f[:, 128:256])
+    smt_out[...] = smt
+    gain = smt[64:65, :]
+
+    for p in range(3):
+        for m in (C, C ^ X, C ^ Y, C ^ Z, C ^ X ^ Y, C ^ X ^ Z, C ^ Y ^ Z, C ^ X ^ Y ^ Z):
+            arrival(p, m).wait_recv()
+    cos_in.wait()
+    sin_in.wait()
+
+    def one_block(r, carry):
+        x = [xg[p, r].astype(f32) for p in range(3)]
+        mean = sum(jnp.sum(t * t, axis=1, keepdims=True) for t in x) * (1.0 / 768)
+        scale = lax.rsqrt(mean + 1e-6)
+        rows = pl.ds(pl.multiple_of(r * 128, 128), 128)
+        acc = jnp.zeros((128, 256), f32)
+        for p in range(3):
+            n = (x[p] * scale * gain[:, 256 * p : 256 * p + 256]).astype(bf16)
+            norm[rows, 256 * p : 256 * p + 256] = n
+            acc = acc + jnp.dot(n, w_b[256 * p : 256 * p + 256, :], preferred_element_type=f32)
+        qk = turned(acc[:, 0:128], cos[rows, :], sin[rows, :])
+        q[rows, :] = (qk[:, 0:64] * 0.125).astype(bf16)
+        k[rows, :] = qk[:, 64:128].astype(bf16)
+        lane = lax.broadcasted_iota(jnp.int32, (128, 128), 1)
+        v[rows, :] = jnp.where(lane < 64, acc[:, 128:256], jnp.where(lane == 64, 1.0, 0.0)).astype(bf16)
+        return carry
+
+    lax.fori_loop(0, 16, one_block, 0)
+    stores = [
+        pltpu.make_async_copy(norm, norm_hbm, loc.at[2]),
+        pltpu.make_async_copy(q, q_hbm, loc.at[3]),
+        pltpu.make_async_copy(k, k_hbm, loc.at[4]),
+        pltpu.make_async_copy(v, v_hbm, loc.at[5]),
+    ]
+    for s in stores:
+        s.start()
+
+    length = lengths[b // 8]
+    head = head_of(h, b)
+    working = (b % 4) != 3
+    base = (b // 8) * 8
+
+    def out_copy(r):
+        return pltpu.make_async_remote_copy(
+            src_ref=sendbuf.at[r], dst_ref=att_in.at[head],
+            send_sem=at_send.at[r], recv_sem=at_recv.at[head],
+            device_id=(r % 2, base + r // 2), device_id_type=MESH,
+        )
+
+    for i in range(8):
+        width = 256 * (i + 1)
+        s = lax.dot_general(q[256 * i : width, :], k[0:width, :], (((1,), (1,)), ((), ())), preferred_element_type=f32)
+        key = lax.broadcasted_iota(jnp.int32, (1, width), 1)
+        s = s + jnp.where(key < length, 0.0, NEG)
+        rowi = lax.broadcasted_iota(jnp.int32, (256, 256), 0)
+        coli = lax.broadcasted_iota(jnp.int32, (256, 256), 1)
+        last = jnp.where(coli <= rowi, s[:, width - 256 :], NEG)
+        s = last if i == 0 else jnp.concatenate([s[:, : width - 256], last], axis=1)
+        m = jnp.max(s, axis=1, keepdims=True)
+        e = jnp.exp(s - m).astype(bf16)
+        ov = jnp.dot(e, v[0:width, :], preferred_element_type=f32)
+        l = ov[:, 64:65]
+        lane = lax.broadcasted_iota(jnp.int32, (256, 128), 1)
+        ov = jnp.where(lane < 64, ov / l, m + jnp.log(l))
+        o[256 * i : width, :] = ov
+        oh = ov[:, 0:64]
+        for half in range(2):
+            r = 2 * i + half
+            packed = jnp.concatenate([oh[128 * half : 128 * half + 64], oh[128 * half + 64 : 128 * half + 128]], axis=1)
+            sendbuf[r] = packed.astype(bf16)
+
+            @pl.when(working & (r != rank))
+            def _(r=r):
+                out_copy(r).start()
+
+    o_store = pltpu.make_async_copy(o, o_hbm, loc.at[6])
+    o_store.start()
+
+    @pl.when(working)
+    def _():
+        att_in[head] = sendbuf[rank]
+
+    for j in range(12):
+        @pl.when(rank != home_of(j))
+        def _(j=j):
+            pltpu.make_async_remote_copy(
+                src_ref=sendbuf.at[0], dst_ref=att_in.at[j],
+                send_sem=at_send.at[0], recv_sem=at_recv.at[j],
+                device_id=(h, b), device_id_type=MESH,
+            ).wait_recv()
+
+    for j in range(0, 12, 2):
+        one, two = att_in[j].astype(f32), att_in[j + 1].astype(f32)
+        att_out[0:64, 64 * j : 64 * j + 128] = jnp.concatenate([one[:, 0:64], two[:, 0:64]], axis=1).astype(bf16)
+        att_out[64:128, 64 * j : 64 * j + 128] = jnp.concatenate([one[:, 64:128], two[:, 64:128]], axis=1).astype(bf16)
+
+    for copy in sends:
+        copy.wait_send()
+
+    def sent_piece(kk, carry):
+        piece_copy(kk).wait_send()
+        return carry
+
+    lax.fori_loop(1, total, sent_piece, 0)
+    for r in range(16):
+        @pl.when(working & (r != rank))
+        def _(r=r):
+            out_copy(r).wait_send()
+    for s in stores:
+        s.wait()
+    o_store.wait()
+
+
+def attend_and_send(tokens, w_qkv, small, lengths, n_blk):
+    cos, sin = rotary_tables(2048)
+    vm = pl.BlockSpec(memory_space=pltpu.VMEM)
+    hbm = pl.BlockSpec(memory_space=pl.ANY)
+    sds = jax.ShapeDtypeStruct
+    DMA = pltpu.SemaphoreType.DMA
+    return pl.pallas_call(
+        functools.partial(forward_kernel, n_blk),
+        out_shape=(
+            sds((2048, 768), bf16), sds((2048, 64), bf16), sds((2048, 64), bf16), sds((2048, 128), bf16),
+            sds((2048, 128), f32), sds((128, 768), bf16), sds((768, 128), f32), sds((128, 768), f32),
+        ),
+        in_specs=[pl.BlockSpec(memory_space=pltpu.SMEM), vm, vm, vm, hbm, hbm],
+        out_specs=(hbm, hbm, hbm, hbm, hbm, vm, vm, vm),
+        scratch_shapes=[
+            pltpu.VMEM((3, 16, 128, 256), bf16), pltpu.VMEM((12, 16, 384), bf16), pltpu.VMEM((2 * n_blk, 16, 384), bf16),
+            pltpu.VMEM((768, 256), f32), pltpu.VMEM((768, 256), bf16),
+            pltpu.VMEM((2048, 128), f32), pltpu.VMEM((2048, 128), f32),
+            pltpu.VMEM((2048, 768), bf16), pltpu.VMEM((2048, 64), bf16), pltpu.VMEM((2048, 64), bf16), pltpu.VMEM((2048, 128), bf16),
+            pltpu.VMEM((2048, 128), f32), pltpu.VMEM((16, 64, 128), bf16), pltpu.VMEM((12, 64, 128), bf16),
+            DMA((3, 16)), DMA((3, 16)), DMA((2 * n_blk,)), DMA((2 * n_blk,)), DMA((16,)), DMA((12,)), DMA((8,)),
+        ],
+        compiler_params=pltpu.CompilerParams(collective_id=0, has_side_effects=True, vmem_limit_bytes=56 * 2**20),
+        cost_estimate=pl.CostEstimate(flops=10**9, bytes_accessed=2 * 10**7, transcendentals=0),
+        name="attend",
+    )(lengths, tokens, w_qkv, small, jnp.asarray(cos), jnp.asarray(sin))
+
+
+def backward_kernel(
+    n_blk, lengths, ag, tok, res_grad, smt, norm_hbm, q_hbm, k_hbm, v_hbm, o_hbm, cos_hbm, sin_hbm, w_hbm,
+    dtok_out, gq_out, gain_out,
+    norm, q, k, v, o, cos, sin, w_all, agbuf, do_in, do, dk, dv, dqkv, obuf, got, dpq, dpv, g_f, gbuf, g_in,
+    a_send, a_recv, b_send, b_recv, g_send, g_recv, loc,
+):
+    h, b = lax.axis_index("head"), lax.axis_index("blk")
+    me = b * 2 + h
+    total = 2 * n_blk
+    _, _, rank = place(0, h, b)
+    base = (b // 8) * 8
+    head = head_of(h, b)
+    working = (b % 4) != 3
+    loads = [
+        pltpu.make_async_copy(src, dst, loc.at[i])
+        for i, (src, dst) in enumerate([
+            (q_hbm, q), (k_hbm, k), (v_hbm, v), (o_hbm, o), (cos_hbm, cos), (sin_hbm, sin), (norm_hbm, norm),
+            (w_hbm, w_all)])
+    ]
+    for c in loads:
+        c.start()
+    a = ag[...].astype(f32)
+    for j in range(12):
+        agbuf[j] = jnp.concatenate([a[0:64, 64 * j : 64 * j + 64], a[64:128, 64 * j : 64 * j + 64]], axis=1).astype(bf16)
+    greet("all", h, b, n_blk)
+
+    def to_head(j):
+        r = home_of(j)
+        return pltpu.make_async_remote_copy(
+            src_ref=agbuf.at[j], dst_ref=do_in.at[rank], send_sem=a_send.at[j], recv_sem=a_recv.at[rank],
+            device_id=(r % 2, base + r // 2), device_id_type=MESH,
+        )
+
+    for j in range(12):
+        @pl.when(rank != home_of(j))
+        def _(j=j):
+            to_head(j).start()
+
+    def to_tokens(r):
+        return pltpu.make_async_remote_copy(
+            src_ref=obuf.at[r], dst_ref=got.at[head], send_sem=b_send.at[r], recv_sem=b_recv.at[head],
+            device_id=(r % 2, base + r // 2), device_id_type=MESH,
+        )
+
+    def to_owner(kk):
+        other = (me + kk) % total
+        oh, ob = other % 2, other // 2
+        return pltpu.make_async_remote_copy(
+            src_ref=gbuf.at[oh * n_blk + ob], dst_ref=g_in.at[me], send_sem=g_send.at[kk], recv_sem=g_recv.at[me],
+            device_id=(oh, ob), device_id_type=MESH,
+        )
+
+    length = lengths[b // 8]
+
+    @pl.when(working)
+    def _():
+        do_in[rank] = agbuf[head]
+        for c in loads[:6]:
+            c.wait()
+
+        def unpack(r, carry):
+            @pl.when(r != rank)
+            def _():
+                pltpu.make_async_remote_copy(
+                    src_ref=agbuf.at[0], dst_ref=do_in.at[r], send_sem=a_send.at[0], recv_sem=a_recv.at[r],
+                    device_id=(h, b), device_id_type=MESH,
+                ).wait_recv()
+
+            t = do_in[r].astype(f32)
+            rows = pl.multiple_of(r * 128, 128)
+            do[pl.ds(rows, 64), :] = t[:, 0:64].astype(bf16)
+            do[pl.ds(rows + 64, 64), :] = t[:, 64:128].astype(bf16)
+            return carry
+
+        lax.fori_loop(0, 16, unpack, 0)
+        for i in range(7, -1, -1):
+            width = 256 * (i + 1)
+            lo = 256 * i
+            qi, doi = q[lo:width, :], do[lo:width, :]
+            s = lax.dot_general(qi, k[0:width, :], (((1,), (1,)), ((), ())), preferred_element_type=f32)
+            key = lax.broadcasted_iota(jnp.int32, (1, width), 1)
+            ov = o[lo:width, :]
+            lse = ov[:, 64:65]
+            s = (s - lse) + jnp.where(key < length, 0.0, NEG)
+            rowi = lax.broadcasted_iota(jnp.int32, (256, 256), 0)
+            coli = lax.broadcasted_iota(jnp.int32, (256, 256), 1)
+            last = jnp.where(coli <= rowi, s[:, lo:], NEG)
+            s = last if i == 0 else jnp.concatenate([s[:, :lo], last], axis=1)
+            p = jnp.exp(s)
+            dp = lax.dot_general(doi, v[0:width, 0:64], (((1,), (1,)), ((), ())), preferred_element_type=f32)
+            inner = jnp.sum(doi.astype(f32) * ov[:, 0:64], axis=1, keepdims=True)
+            ds = (p * (dp - inner)).astype(bf16)
+            p = p.astype(bf16)
+            dq = jnp.dot(ds, k[0:width, :], preferred_element_type=f32) * 0.125
+            dki = lax.dot_general(ds, qi, (((0,), (0,)), ((), ())), preferred_element_type=f32)
+            dvi = lax.dot_general(p, doi, (((0,), (0,)), ((), ())), preferred_element_type=f32)
+            if i == 7:
+                dk[...] = dki
+                dv[...] = dvi
+            else:
+                dk[0:width, :] += dki
+                dv[0:width, :] += dvi
+            both = jnp.concatenate([dq, dk[lo:width, :]], axis=1)
+            both = turned(both, cos[lo:width, :], -sin[lo:width, :]).astype(bf16)
+            dvl = dv[lo:width, :]
+            dqkv[lo:width, 0:128] = both
+            dqkv[lo:width, 128:256] = jnp.concatenate([dvl, jnp.zeros_like(dvl)], axis=1).astype(bf16)
+            for half in range(2):
+                r = 2 * i + half
+                obuf[r, 0:128, :] = both[128 * half : 128 * half + 128]
+                obuf[r, 128:192, :] = jnp.concatenate(
+                    [dvl[128 * half : 128 * half + 64], dvl[128 * half + 64 : 128 * half + 128]], axis=1).astype(bf16)
+
+                @pl.when(r != rank)
+                def _(r=r):
+                    to_tokens(r).start()
+
+        got[head] = obuf[rank]
+        loads[6].wait()
+        for c in range(3):
+            g_f[256 * c : 256 * c + 256, :] = lax.dot_general(
+                norm[:, 256 * c : 256 * c + 256], dqkv[...], (((0,), (0,)), ((), ())), preferred_element_type=f32)
+        for w in range(total):
+            t = g_f[24 * w : 24 * w + 24, :]
+            gbuf[w, :, 0:256] = t[0:16].astype(bf16)
+            gbuf[w, :, 256:384] = jnp.concatenate([t[16:24, 0:128], t[16:24, 128:256]], axis=0).astype(bf16)
+
+        def send_g(kk, carry):
+            to_owner(kk).start()
+            return carry
+
+        lax.fori_loop(1, total, send_g, 0)
+        g_in[me] = gbuf[h * n_blk + b]
+
+    @pl.when(jnp.logical_not(working))
+    def _():
+        for c in loads[:7]:
+            c.wait()
+
+    for j in range(12):
+        @pl.when(rank != home_of(j))
+        def _(j=j):
+            pltpu.make_async_remote_copy(
+                src_ref=obuf.at[0], dst_ref=got.at[j], send_sem=b_send.at[0], recv_sem=b_recv.at[j],
+                device_id=(h, b), device_id_type=MESH,
+            ).wait_recv()
+    for j in range(0, 12, 2):
+        dpq[:, 128 * j : 128 * j + 128] = got[j, 0:128, :]
+        dpq[:, 128 * j + 128 : 128 * j + 256] = got[j + 1, 0:128, :]
+        one, two = got[j, 128:192, :].astype(f32), got[j + 1, 128:192, :].astype(f32)
+        dpv[0:64, 64 * j : 64 * j + 128] = jnp.concatenate([one[:, 0:64], two[:, 0:64]], axis=1).astype(bf16)
+        dpv[64:128, 64 * j : 64 * j + 128] = jnp.concatenate([one[:, 64:128], two[:, 64:128]], axis=1).astype(bf16)
+    loads[7].wait()
+    dn = lax.dot_general(dpq[...], w_all[:, 0:1536], (((1,), (1,)), ((), ())), preferred_element_type=f32)
+    dn = dn + lax.dot_general(dpv[...], w_all[:, 1536:2304], (((1,), (1,)), ((), ())), preferred_element_type=f32)
+    x = tok[...].astype(f32)
+    scale = lax.rsqrt(jnp.sum(x * x, axis=1, keepdims=True) * (1.0 / 768) + 1e-6)
+    xh = x * scale
+    gain_out[...] = jnp.broadcast_to(jnp.sum(dn * xh, axis=0, keepdims=True), (8, 768))
+    t = dn * smt[64:65, :]
+    dx = scale * (t - xh * (jnp.sum(t * xh, axis=1, keepdims=True) * (1.0 / 768)))
+    dtok_out[...] = (res_grad[...] + dx).astype(bf16)
+
+    for src in range(total):
+        if (src // 2) % 4 == 3:
+            continue
+
+        @pl.when(me != src)
+        def _(src=src):
+            pltpu.make_async_remote_copy(
+                src_ref=gbuf.at[0], dst_ref=g_in.at[src], send_sem=g_send.at[0], recv_sem=g_recv.at[src],
+                device_id=(h, b), device_id_type=MESH,
+            ).wait_recv()
+    for j in range(0, 12, 2):
+        pair = []
+        for jj in (j, j + 1):
+            t = sum(g_in[16 * s + home_of(jj)].astype(f32) for s in range(total // 16))
+            pair.append(jnp.concatenate(
+                [t[:, 0:256], jnp.concatenate([t[0:8, 256:384], t[8:16, 256:384]], axis=1)], axis=0))
+        one, two = pair
+        for part in range(3):
+            gq_out[:, 768 * part + 64 * j : 768 * part + 64 * j + 128] = jnp.concatenate(
+                [one[:, 64 * part : 64 * part + 64], two[:, 64 * part : 64 * part + 64]], axis=1)
+
+    for j in range(12):
+        @pl.when(rank != home_of(j))
+        def _(j=j):
+            to_head(j).wait_send()
+
+    @pl.when(working)
+    def _():
+        for r in range(16):
+            @pl.when(r != rank)
+            def _(r=r):
+                to_tokens(r).wait_send()
+
+        def sent(kk, carry):
+            to_owner(kk).wait_send()
+            return carry
+
+        lax.fori_loop(1, total, sent, 0)
+
+
+def attend_back(lengths, ag, tok, res_grad, smt, norm, q, k, v, o, w_all, n_blk):
+    cos, sin = rotary_tables(2048)
+    vm = pl.BlockSpec(memory_space=pltpu.VMEM)
+    hbm = pl.BlockSpec(memory_space=pl.ANY)
+    sds = jax.ShapeDtypeStruct
+    DMA = pltpu.SemaphoreType.DMA
+    V = pltpu.VMEM
+    total = 2 * n_blk
+    return pl.pallas_call(
+        functools.partial(backward_kernel, n_blk),
+        out_shape=(sds((128, 768), bf16), sds((24, 2304), f32), sds((8, 768), f32)),
+        in_specs=[pl.BlockSpec(memory_space=pltpu.SMEM), vm, vm, vm, vm] + [hbm] * 8,
+        out_specs=(vm, vm, vm),
+        scratch_shapes=[
+            V((2048, 768), bf16), V((2048, 64), bf16), V((2048, 64), bf16), V((2048, 128), bf16), V((2048, 128), f32),
+            V((2048, 128), f32), V((2048, 128), f32), V((768, 2304), bf16),
+            V((12, 64, 128), bf16), V((16, 64, 128), bf16), V((2048, 64), bf16), V((2048, 64), f32), V((2048, 64), f32),
+            V((2048, 256), bf16), V((16, 192, 128), bf16), V((12, 192, 128), bf16), V((128, 1536), bf16), V((128, 768), bf16),
+            V((768, 256), f32), V((total, 16, 384), bf16), V((total, 16, 384), bf16),
+            DMA((12,)), DMA((16,)), DMA((16,)), DMA((12,)), DMA((total,)), DMA((total,)), DMA((8,)),
+        ],
+        compiler_params=pltpu.CompilerParams(collective_id=1, has_side_effects=True, vmem_limit_bytes=56 * 2**20),
+        cost_estimate=pl.CostEstimate(flops=2 * 10**9, bytes_accessed=2 * 10**7, transcendentals=0),
+        name="attend_back",
+    )(lengths, ag, tok, res_grad, smt, norm, q, k, v, o, jnp.asarray(cos), jnp.asarray(sin), w_all)
+
+
 CAP = 24
 
 
@@ -449,9 +1001,136 @@
     )
 
 
+def on_device_small(
+    tokens, cotangent, prev_logits, routes, lengths, w_qkv, w_out, w_router, w_const, const_vec, norm_gains, gate_mix,
+    expert_weights,
+):
+    tok_dev, model_width = tokens.shape
+    head_count, blk_count = lax.axis_size("head"), lax.axis_size("blk")
+    head_index, blk_index = lax.axis_index("head"), lax.axis_index("blk")
+    slot_size = 8 * head_count * tok_dev
+    both = ("head", "blk")
+    small = jnp.concatenate(
+        [norm_gains, w_router, w_const, const_vec, jnp.zeros((24, 44), bf16)], axis=1).astype(f32)
+    out_w = lax.all_gather(w_out, both, axis=0, tiled=True)
+    w_local = w_qkv.reshape(24, 3, 12, 64)
+    w_local = jnp.concatenate(
+        [w_local[:, :2].transpose(0, 2, 1, 3).reshape(24, 1536), w_qkv[:, 1536:]], axis=1)
+    w_all = lax.all_gather(w_local, both, axis=0, tiled=True)
+    norm, q, k, v, o, attended_tok, sm, smt = attend_and_send(tokens, w_qkv, small, lengths, blk_count)
+    router_w, const_w, vector_w = sm[:, 66:78], sm[:, 78:82], sm[:, 82:84]
+    gain_two = smt[65]
+    row_ids = (blk_index * head_count + head_index) * tok_dev + jnp.arange(tok_dev, dtype=jnp.int32)
+    slot_ids = row_ids // slot_size
+    positions = row_ids - slot_ids * slot_size
+    live_rows = (positions < slot_lengths(slot_ids, lengths)).astype(f32)
+    inputs = tokens.astype(f32)
+    residual = inputs + jnp.dot(attended_tok, out_w, preferred_element_type=f32)
+    normed_two, norm_two_back = jax.vjp(rms_norm, residual, gain_two)
+    normed_two_low = normed_two.astype(bf16)
+    normed_two_f = normed_two_low.astype(f32)
+    router_prob, router_back = jax.vjp(
+        partial(router_probs, prev_scores=prev_logits), normed_two_f, router_w, gate_mix)
+    expert_count = 12
+    real_count = expert_weights.shape[1] * head_count
+    choose = (routes[:, :, None] == jnp.arange(expert_count, dtype=jnp.int32)[None, None, :]).astype(f32)
+    count_local = jnp.sum(jnp.sum(choose, axis=1) * live_rows[:, None], axis=0)
+    prob_local = jnp.sum(router_prob * live_rows[:, None], axis=0)
+    count_all, prob_all = lax.psum((count_local, prob_local), both)
+    live_total = jnp.sum(lengths).astype(f32)
+    fraction = count_all / (2.0 * live_total)
+    aux_loss = expert_count * jnp.sum(fraction * (prob_all / live_total))
+    gate_values = jnp.sum(choose * router_prob[:, None, :], axis=-1)
+    out_grad = live_rows[:, None] * cotangent.astype(f32)
+    assigned = routes.reshape(-1)
+    live_pairs = jnp.repeat(live_rows, 2)
+    is_real = (assigned < real_count) & (live_pairs > 0)
+    onehot = (
+        (assigned[:, None] == jnp.arange(real_count, dtype=jnp.int32)[None, :]) & is_real[:, None]
+    ).astype(jnp.int32)
+    slot_rank = jnp.sum((jnp.cumsum(onehot, axis=0) - onehot) * onehot, axis=1)
+    target = jnp.where(is_real, assigned * CAP + slot_rank, real_count * CAP)
+    source = (
+        jnp.full((real_count * CAP + 1,), 2 * tok_dev, jnp.int32)
+        .at[target]
+        .set(jnp.arange(2 * tok_dev, dtype=jnp.int32))[: real_count * CAP]
+    )
+    zero_row = jnp.zeros((1, model_width), bf16)
+    send_rows = jnp.concatenate([normed_two_low, zero_row], axis=0)[source // 2].reshape(real_count, CAP, model_width)
+    pair_grads = (gate_values.reshape(-1, 1) * jnp.repeat(out_grad, 2, axis=0)).astype(bf16)
+    send_grads = jnp.concatenate([pair_grads, zero_row], axis=0)[source].reshape(real_count, CAP, model_width)
+    expert_in, expert_cot = (
+        lax.all_to_all(send_rows, "head", split_axis=0, concat_axis=1, tiled=True),
+        lax.all_to_all(send_grads, "head", split_axis=0, concat_axis=1, tiled=True),
+    )
+    rows_in = lax.all_gather(expert_in, "blk", axis=1, tiled=True)
+    rows_cot = lax.all_gather(expert_cot, "blk", axis=1, tiled=True)
+    gate_w = expert_weights[:, :, 0, :]
+    up_w = expert_weights[:, :, 1, :]
+    down_w = expert_weights[:, :, 2, :]
+    gate_part = jnp.einsum("esd,ned->esn", rows_in, gate_w, preferred_element_type=f32)
+    up_part = jnp.einsum("esd,ned->esn", rows_in, up_w, preferred_element_type=f32)
+    sigmoid_part = jax.nn.sigmoid(gate_part)
+    silu_part = gate_part * sigmoid_part
+    hidden = (silu_part * up_part).astype(bf16)
+    hidden_grad = jnp.einsum("esd,ned->esn", rows_cot, down_w, preferred_element_type=f32)
+    gate_grad = (hidden_grad * up_part * (sigmoid_part * (1.0 + gate_part * (1.0 - sigmoid_part)))).astype(bf16)
+    up_grad = (hidden_grad * silu_part).astype(bf16)
+    in_grad = jnp.einsum("esn,ned->esd", gate_grad, gate_w, preferred_element_type=f32)
+    in_grad = in_grad + jnp.einsum("esn,ned->esd", up_grad, up_w, preferred_element_type=f32)
+    in_grad = lax.psum_scatter(in_grad.astype(bf16), "blk", scatter_dimension=1, tiled=True)
+    out_sum = jnp.einsum("esn,ned->esd", hidden, down_w, preferred_element_type=f32)
+    out_sum = lax.psum_scatter(out_sum.astype(bf16), "blk", scatter_dimension=1, tiled=True)
+    gate_w_grad = jnp.einsum("esn,esd->ned", gate_grad, rows_in, preferred_element_type=f32)
+    up_w_grad = jnp.einsum("esn,esd->ned", up_grad, rows_in, preferred_element_type=f32)
+    down_w_grad = jnp.einsum("esn,esd->ned", hidden, rows_cot, preferred_element_type=f32)
+    expert_grads = jnp.stack([gate_w_grad, up_w_grad, down_w_grad], axis=2)
+    returned, returned_grad = (
+        lax.all_to_all(out_sum, "head", split_axis=1, concat_axis=0, tiled=True),
+        lax.all_to_all(in_grad, "head", split_axis=1, concat_axis=0, tiled=True),
+    )
+    outputs_pair = (
+        jnp.concatenate([returned.reshape(-1, model_width), zero_row], axis=0)[target]
+        .astype(f32).reshape(tok_dev, 2, model_width)
+    )
+    input_pair = (
+        jnp.concatenate([returned_grad.reshape(-1, model_width), zero_row], axis=0)[target]
+        .astype(f32).reshape(tok_dev, 2, model_width)
+    )
+    expert_input_grad = input_pair[:, 0] + input_pair[:, 1]
+    branch, branch_back = jax.vjp(
+        partial(branch_sum, choose=choose, live_rows=live_rows, real_count=real_count),
+        router_prob, normed_two_f, const_w, vector_w, outputs_pair)
+    output = ((residual + branch) * live_rows[:, None]).astype(bf16)
+    prob_grad, normed_grad_branch, const_grad, vector_grad, unused_grad = branch_back(out_grad)
+    aux_grad = aux_weight * expert_count / live_total * fraction[None, :] * live_rows[:, None]
+    normed_grad_router, router_grad, mixing_grad = router_back(prob_grad + aux_grad)
+    normed_grad = normed_grad_router + normed_grad_branch + expert_input_grad
+    residual_grad_norm, gain_two_grad = norm_two_back(normed_grad)
+    residual_grad = out_grad + residual_grad_norm
+    residual_grad_low = residual_grad.astype(bf16)
+    out_w_grad = jnp.dot(attended_tok.T, residual_grad_low, preferred_element_type=f32)
+    attended_grad = jnp.dot(residual_grad_low, out_w.T, preferred_element_type=f32).astype(bf16)
+    token_grad, qkv_grad, gain_one = attend_back(
+        lengths, attended_grad, tokens, residual_grad, smt, norm, q, k, v, o, w_all, blk_count)
+    weight_grads = (
+        lax.psum_scatter(out_w_grad, both, scatter_dimension=0, tiled=True),
+        lax.psum_scatter(
+            jnp.concatenate([router_grad, const_grad, vector_grad, gain_one[0][:, None], gain_two_grad[:, None]], axis=1),
+            both, scatter_dimension=0, tiled=True),
+    )
+    mixing_total = lax.psum(mixing_grad, both)
+    tail = weight_grads[1]
+    return (
+        output, aux_loss, token_grad, qkv_grad, weight_grads[0], tail[:, 0:12], tail[:, 12:16], tail[:, 16:18],
+        tail[:, 18:20], mixing_total, expert_grads,
+    )
+
+
 def solution(mesh):
+    small = mesh.shape["blk"] == 16 and mesh.shape["head"] == 2
     return jax.shard_map(
-        on_device,
+        on_device_small if small else on_device,
         mesh=mesh,
         in_specs=(
             P(("blk", "head"), None),

time: 935 us -> 543 us (0.58)
  blocking collectives: 283 us -> 96.9 us
  starting transfers between devices: 156 us -> 18 us
  waiting for transfers between devices: 112 us -> 221 us
  matrix products: 148 us -> 42.8 us
  local copies, waits for them, and re-layouts: 126 us -> 40.7 us
  Pallas kernels: 0 us -> 84.3 us
  other arithmetic: 57.5 us -> 12.7 us
  loops' own time: 20.5 us -> 0 us
    all_gather x4 -> x0, blocking collectives: 195 us -> none  [the longest x1 75.9 us: on_device(): lax.all_gather(const_vec, ('head', 'blk'), axis=0, tiled=True)]
    reduce_scatter x2 -> x3, waiting for transfers between devices: 0.01 us -> 133 us  [the longest x1 74.1 us: on_device_small(): lax.psum_scatter(in_grad.astype(bf16), 'blk', scatter_dimension=1, tiled=...]
    dot_general x57 -> x12, matrix products: 143 us -> 37.5 us  [the longest x1 6.18 us: on_device_small(): jnp.einsum('esd,ned->esn', rows_cot, down_w, preferred_element_type=f32)]
    pallas_call x0 -> x2, Pallas kernels: none -> 84.3 us  [the longest x1 46.9 us: attend_and_send(): pl.pallas_call(functools.partial(forward_kernel, n_blk), out_shape=(sds((...]
    all_gather x5 -> x4, waiting for transfers between devices: 8.62 us -> 87.3 us  [the longest x1 46.7 us: on_device_small(): rows_cot = lax.all_gather(expert_cot, 'blk', axis=1, tiled=True)]
    ppermute x28 -> x0, starting transfers between devices: 78.5 us -> none  [shifted(): return lax.ppermute(block, axis, route)]
    all_to_all x14 -> x2, starting transfers between devices: 76.7 us -> 6.91 us  [the longest x1 3.46 us: on_device_small(): lax.all_to_all(in_grad, 'head', split_axis=1, concat_axis=0, tiled=True)]
    all_to_all x14 -> x2, waiting for transfers between devices: 52.7 us -> 0.01 us  [the longest x1 0.01 us: on_device_small(): lax.all_to_all(out_sum, 'head', split_axis=1, concat_axis=0, tiled=True)]
  transfers between devices with their start and end apart: 49 -> 9, of which waited for: 18 -> 6; matrix products, arithmetic and copies ran while one was open for 36% -> 15% of each run, Pallas kernels for 0% -> 16%
where the time goes in v1:
time: 543 us; the launch traced here: 534 us
  waiting for transfers between devices  221 us (41%)
  blocking collectives  96.9 us (18%)
  Pallas kernels  84.3 us (16%)
  matrix products  42.8 us (8%)
  local copies, waits for them, and re-layouts  40.7 us (7%)
  starting transfers between devices  18 us (3%)
  between operations  17.7 us (3%)
  other arithmetic  12.7 us (2%)
    psum x2, blocking collectives, on_device_small(): count_all, prob_all = lax.psum((count_local, prob_local), both)  80.3 us
    reduce_scatter x1, waiting for transfers between devices, on_device_small(): lax.psum_scatter(in_grad.astype(bf16), 'blk', scatter_dimension=1, tiled=...  74.1 us
    reduce_scatter x1, waiting for transfers between devices, on_device_small(): lax.psum_scatter(out_sum.astype(bf16), 'blk', scatter_dimension=1, tiled=...  54.4 us
    pallas_call x1, Pallas kernels, attend_and_send(): pl.pallas_call(functools.partial(forward_kernel, n_blk), out_shape=(sds((...  46.9 us
    all_gather x1, waiting for transfers between devices, on_device_small(): rows_cot = lax.all_gather(expert_cot, 'blk', axis=1, tiled=True)  46.7 us
    pallas_call x1, Pallas kernels, attend_back(): pl.pallas_call(functools.partial(backward_kernel, n_blk), out_shape=(sds(...  37.4 us
    all_gather x1, waiting for transfers between devices, on_device_small(): rows_in = lax.all_gather(expert_in, 'blk', axis=1, tiled=True)  34.3 us
    unnamed x61, local copies, waits for them, and re-layouts  15.8 us
  transfers between devices with their start and end apart: 9, of which 6 were waited for; matrix products, arithmetic and copies ran while one was open for 15% of the time, Pallas kernels for 16%

profile of v1, /device:TPU:0, one launch (start us, length us, event | category | flops | bytes accessed | tf_op | source)
XLA Modules:
  0.0 534.1 jit_solution(1599928780335719510)
XLA Ops:
  8.0 0.8 copy.152
  9.8 0.8 copy.146
  10.6 0.8 copy.147
  17.1 1.4 scatter_custom_fusion
  18.5 46.9 %attend.1 = (bf16[2048,768]{1,0:T(8,128)(2,1)}, bf16[2048,64]{1,0:T(8,128)(2,1)}, bf16[2048,64]{1,0:T(8,128)(2,1)}, bf16[2048,128]{1,0:T(8,128)(2,1)}, f32[2048,...) custom-call(s32[2]{0:T(128)} %lengths.3, bf16[128,768]{1,0:T(8,128)(2,1)} %tok.3, ...), custom_call_target="tpu_custom_call" | custom-call | flops 1000000000 | bytes 20000000 | tf_op jit(solution)/shard_map/attend/pallas_call | solution.py:311
  66.2 6.3 %all-gather.5.cloned.1.call-done = bf16[768,768]{1,0:T(8,128)(2,1)} async-done(((bf16[24,768]{1,0:T(8,128)(2,1)}), bf16[768,768]{1,0:T(8,128)(2,1)}) %all-gather.5.cloned.1.call-update) | async-done | bytes 1179664 | tf_op jit(solution)/shard_map/all_gather | solution.py:1015
  72.5 1.8 multiply_reduce_fusion.10
  74.8 1.0 gather_fusion
  75.9 8.7 %all_to_all.66 = bf16[8,24,768]{2,1,0:T(8,128)(2,1)S(1)} all-to-all(bf16[8,24,768]{2,1,0:T(8,128)(2,1)S(1)} %bitcast.120), channel_id=1, replica_groups=mesh['head'=2,'blk'=16] {'head'}, dimensions={0} | all-to-all | bytes 589824 | tf_op jit(solution)/shard_map/all_to_all | solution.py:1063
  89.7 1.0 gather_fusion.2
  90.7 7.8 %all_to_all.67 = bf16[8,24,768]{2,1,0:T(8,128)(2,1)S(1)} all-to-all(bf16[8,24,768]{2,1,0:T(8,128)(2,1)S(1)} %bitcast.121), channel_id=1, replica_groups=mesh['head'=2,'blk'=16] {'head'}, dimensions={0} | all-to-all | bytes 589824 | tf_op jit(solution)/shard_map/all_to_all | solution.py:1064
  99.3 3.3 fusion.47
  102.7 34.3 %all-gather.7.cloned.1.call-done = bf16[4,768,768]{2,1,0:T(8,128)(2,1)} async-done(((bf16[4,48,768]{2,1,0:T(8,128)(2,1)}), bf16[4,768,768]{2,1,0:T(8,128)(2,1)}) %all-gather.7.cloned.1.call-update) | async-done | bytes 4718608 | tf_op jit(solution)/shard_map/all_gather | solution.py:1066
  137.0 5.0 fusion.7
  142.0 2.5 fusion.8
  144.5 46.7 %all-gather.9.cloned.1.call-done = bf16[4,768,768]{2,1,0:T(8,128)(2,1)} async-done(((bf16[4,48,768]{2,1,0:T(8,128)(2,1)}), bf16[4,768,768]{2,1,0:T(8,128)(2,1)}) %all-gather.9.cloned.1.call-update) | async-done | bytes 4718608 | tf_op jit(solution)/shard_map/all_gather | solution.py:1067
  191.2 6.2 %multiply_convert_fusion = (bf16[4,768,128]{2,1,0:T(8,128)(2,1)}, bf16[4,768,128]{2,1,0:T(8,128)(2,1)S(1)}, bf16[4,768,128]{2,1,0:T(8,128)(2,1)S(1)}) fusion(f32[4,768,128]{2,1,0:T(8,128)} %fusion.7, f32[4,768,128]{2,1,0:T(8,128)} %fusion.8, bf16[4,768,768]{2,1,0:T(8,128)(2,1)} %all-gather.9.cloned.1.call-done, bf16[128,4,1,768]{3,1,2,0:T(4,128)(2,1)} %get-tuple-element.128), kind=kOutput, calls=%fused_computation.9 | convolution fusion | flops 609878016 | bytes 11010048 | tf_op jit(solution)/shard_map/esd,ned->esn/dot_general | solution.py:1076
  197.4 0.9 copy-done.5
  198.3 3.6 convolution_convert_fusion
  202.0 1.4 fusion.6
  203.4 3.6 add_convert_fusion
  207.0 10.5 %all-gather.11.cloned.1.call-start = ((), (), s32[]{:S(2)}) async-start(), calls=%async_computation.12 | async-start | bytes 3649536 | tf_op jit(solution)/shard_map/all_gather | solution.py:1019
  220.2 1.5 fusion.3
  221.8 54.4 %reduce-scatter.5.cloned.1.call-done = bf16[4,48,768]{2,1,0:T(8,128)(2,1)} async-done(((bf16[4,768,768]{2,1,0:T(8,128)(2,1)}), bf16[4,48,768]{2,1,0:T(8,128)(2,1)}) %reduce-scatter.5.cloned.1.call-update) | async-done | bytes 294928 | tf_op jit(solution)/shard_map/reduce_scatter | solution.py:1083
  276.2 1.8 copy.159
  278.0 3.4 all-to-all-start.1
  281.5 74.1 %reduce-scatter.7.cloned.1.call-done = bf16[4,48,768]{2,1,0:T(8,128)(2,1)} async-done(((bf16[4,768,768]{2,1,0:T(8,128)(2,1)}), bf16[4,48,768]{2,1,0:T(8,128)(2,1)}) %reduce-scatter.7.cloned.1.call-update) | async-done | bytes 294928 | tf_op jit(solution)/shard_map/reduce_scatter | solution.py:1081
  355.6 1.8 copy.164
  357.5 1.9 gather_fusion.1
  359.4 1.4 reshape.306
  360.8 2.1 multiply_reduce_fusion
  363.1 3.5 all-to-all-start.3
  366.6 40.2 %psum.21 = f32[12]{0:T(128)S(1)} all-reduce(f32[12]{0:T(128)S(1)} %multiply_reduce_fusion.13), channel_id=1, replica_groups=mesh['head'=2,'blk'=16] {'head','blk'}, use_global_device_ids=true, to_apply=%region_16.17 | all-reduce | flops 12 | bytes 96 | tf_op jit(solution)/shard_map/psum | solution.py:1039
  407.1 1.2 gather_fusion.3
  409.4 1.9 multiply_reduce_fusion.2
  411.3 1.1 fusion.10
  412.4 1.9 fusion.31
  414.6 4.4 convolution_bitcast_fusion
  419.0 4.1 convolution_bitcast_fusion.1
  423.1 1.8 convolution_bitcast_fusion.2
  424.9 2.5 pad_maximum_fusion
  427.4 6.7 %copy.170 = f32[128,4,3,768]{3,1,2,0:T(4,128)} copy(f32[128,4,3,768]{0,3,1,2:T(8,128)} %pad_maximum_fusion) | data formatting | bytes 9437184
  434.2 1.2 convolution_convert_fusion.1.ag
  435.4 37.4 %attend_back.1 = (bf16[128,768]{1,0:T(8,128)(2,1)}, f32[24,2304]{1,0:T(8,128)}, f32[8,768]{1,0:T(8,128)}) custom-call(s32[2]{0:T(128)} %lengths.3, bf16[128,768]{1,0:T(8,128)(2,1)} %convolution_convert_fusion.1.ag, bf16[128,768]{1,0:T(8,128)(2,1)} %tok.3, f32[128,768]{1,0:T(8,128)} %copy-done.3, f32[128,768]{1,0:T(8,128)} %get-tuple-element.23.smt, ...), custom_call_target="tpu_custom_call" | custom-call | flops 2000000000 | bytes 20000000 | tf_op jit(solution)/shard_map/attend_back/pallas_call | solution.py:544
  473.9 40.1 %all-reduce.14 = (f32[12]{0:T(128)S(1)}, f32[768,20]{0,1:T(8,128)S(1)}, f32[12,12]{0,1:T(8,128)S(1)}) all-reduce(f32[12]{0:T(128)S(1)} %get-tuple-element.117, f32[768,20]{0,1:T(8,128)S(1)} %concatenate.27, f32[12,12]{0,1:T(8,128)S(1)} %convolution_bitcast_fusion.3), channel_id=1, replica_groups=mesh['head'=2,'blk'=16] {'head','blk'}, use_global_device_ids=true, to_apply=%region_19.20 | all-reduce | flops 15516 | bytes 124128 | tf_op jit(solution)/shard_map/psum | solution.py:1039
  517.9 4.6 reduce-scatter.9.cloned.1.call-done
  522.5 1.6 copy.197
  524.1 1.6 copy.198
  (173 shorter events, 22.7 us)
Async XLA Ops:
  7.2 79.6 %copy-start = (f32[128,12]{0,1:T(8,128)S(1)}, f32[128,12]{0,1:T(8,128)}, u32[]{:S(2)}) copy-start(f32[128,12]{0,1:T(8,128)} %param.19) | copy-start | bytes 18436
  7.2 65.3 %copy-start.17 = (bf16[128,768]{1,0:T(8,128)(2,1)S(1)}, bf16[128,768]{1,0:T(8,128)(2,1)}, u32[]{:S(2)}) copy-start(bf16[128,768]{1,0:T(8,128)(2,1)} %tok.3) | copy-start | bytes 589828
  7.2 65.3 %all-gather.5.cloned.1.call-start = ((), (), s32[]{:S(2)}) async-start(), calls=%async_computation.7 | async-start | bytes 1216512 | tf_op jit(solution)/shard_map/all_gather | solution.py:1015
  7.9 129.0 %all-gather.7.cloned.1.call-start = ((), (), s32[]{:S(2)}) async-start(), calls=%async_computation.8 | async-start | bytes 5013504 | tf_op jit(solution)/shard_map/all_gather | solution.py:1066
  74.3 0.5 copy-start.21
  74.4 11.2 %copy-start.2 = (f32[768,128]{1,0:T(8,128)S(1)}, f32[768,128]{1,0:T(8,128)}, u32[]{:S(2)}) copy-start(f32[768,128]{1,0:T(8,128)} %get-tuple-element.24) | copy-start | bytes 1179652
  74.8 11.9 %copy-start.23 = (f32[12,12]{1,0:T(8,128)S(1)}, f32[12,12]{1,0:T(8,128)}, u32[]{:S(2)}) copy-start(f32[12,12]{1,0:T(8,128)} %param.28) | copy-start | bytes 1732
  74.8 12.2 %copy-start.19 = (s32[128,2]{0,1:T(2,128)S(1)}, s32[128,2]{0,1:T(2,128)}, u32[]{:S(2)}) copy-start(s32[128,2]{0,1:T(2,128)} %param.20) | copy-start | bytes 3076
  75.8 12.0 %copy-start.14 = (bf16[128,768]{1,0:T(8,128)(2,1)S(1)}, bf16[128,768]{1,0:T(8,128)(2,1)}, u32[]{:S(2)}) copy-start(bf16[128,768]{1,0:T(8,128)(2,1)} %param.18) | copy-start | bytes 589828
  85.4 105.9 %all-gather.9.cloned.1.call-start = ((), (), s32[]{:S(2)}) async-start(), calls=%async_computation.10 | async-start | bytes 5013504 | tf_op jit(solution)/shard_map/all_gather | solution.py:1067
  99.3 176.9 %reduce-scatter.5.cloned.1.call-start = ((), (), s32[]{:S(2)}) async-start(), calls=%async_computation.9 | async-start | bytes 5013504 | tf_op jit(solution)/shard_map/reduce_scatter | solution.py:1083
  102.7 39.3 %copy-start.10 = (bf16[128,4,1,768]{3,1,2,0:T(4,128)(2,1)}, bf16[128,4,1,768]{3,1,2,0:T(4,128)(2,1)S(1)}, u32[]{:S(2)}) copy-start(bf16[128,4,1,768]{3,1,2,0:T(4,128)(2,1)S(1)} %get-tuple-element.129) | copy-start | bytes 2359300
  137.0 5.0 copy-start.1
  191.2 7.1 %copy-start.7 = (bf16[128,4,1,768]{3,1,2,0:T(4,128)(2,1)S(1)}, bf16[128,4,1,768]{3,1,2,0:T(4,128)(2,1)}, u32[]{:S(2)}) copy-start(bf16[128,4,1,768]{3,1,2,0:T(4,128)(2,1)} %get-tuple-element.128) | copy-start | bytes 2359300
  197.4 0.9 copy-start.5
  201.9 153.6 %reduce-scatter.7.cloned.1.call-start = ((), (), s32[]{:S(2)}) async-start(), calls=%async_computation.11 | async-start | bytes 5013504 | tf_op jit(solution)/shard_map/reduce_scatter | solution.py:1081
  202.0 1.4 copy-start.8
  202.0 1.4 copy-start.11
  207.0 10.6 %copy-start.18 = (bf16[24,2304]{1,0:T(8,128)(2,1)S(1)}, bf16[24,2304]{1,0:T(8,128)(2,1)}, u32[]{:S(2)}) copy-start(bf16[24,2304]{1,0:T(8,128)(2,1)} %w_in.1) | copy-start | bytes 331780
  207.0 11.1 %slice-start.2 = ((bf16[24,2304]{1,0:T(8,128)(2,1)}), bf16[24,768]{1,0:T(8,128)(2,1)S(1)}, s32[]{:S(2)}) async-start(bf16[24,2304]{1,0:T(8,128)(2,1)} %w_in.1), calls=%async_computation.16 | async-start | bytes 73728 | tf_op jit(solution)/shard_map/slice | solution.py:1018
  207.0 11.8 %copy-start.20 = (s32[2]{0:T(128)S(1)}, s32[2]{0:T(128)}, u32[]{:S(2)}) copy-start(s32[2]{0:T(128)} %lengths.3) | copy-start | bytes 28
  207.0 13.3 %copy-start.15 = (bf16[128,768]{1,0:T(8,128)(2,1)S(1)}, bf16[128,768]{1,0:T(8,128)(2,1)}, u32[]{:S(2)}) copy-start(bf16[128,768]{1,0:T(8,128)(2,1)} %param.18) | copy-start | bytes 589828
  207.0 228.4 %all-gather.11.cloned.1.call-start = ((), (), s32[]{:S(2)}) async-start(), calls=%async_computation.12 | async-start | bytes 3649536 | tf_op jit(solution)/shard_map/all_gather | solution.py:1019
  278.0 79.4 %all-to-all-start.1 = ((bf16[4,48,768]{2,0,1:T(4,128)(2,1)}), bf16[4,48,768]{2,0,1:T(4,128)(2,1)S(1)}, u32[]{:S(2)}, u32[]{:S(2)}) async-start(bf16[4,48,768]{2,0,1:T(4,128)(2,1)} %copy.159), calls=%async_computation.2 | async-start | bytes 589824 | tf_op jit(solution)/shard_map/all_to_all | solution.py:1089
  363.1 43.9 %all-to-all-start.3 = ((bf16[4,48,768]{2,0,1:T(4,128)(2,1)}), bf16[4,48,768]{2,0,1:T(4,128)(2,1)S(1)}, u32[]{:S(2)}, u32[]{:S(2)}) async-start(bf16[4,48,768]{2,0,1:T(4,128)(2,1)} %copy.164), calls=%async_computation.5 | async-start | bytes 589824 | tf_op jit(solution)/shard_map/all_to_all | solution.py:1090
  366.6 155.9 %reduce-scatter.9.cloned.1.call-start = ((), (), s32[]{:S(2)}) async-start(), calls=%async_computation.13 | async-start | bytes 2433024 | tf_op jit(solution)/shard_map/reduce_scatter | solution.py:1117
  408.3 3.0 copy-start.22
  408.3 3.0 copy-start.12
  408.7 2.6 copy-start.16
  409.4 3.0 copy-start.13
  412.4 21.7 %copy-start.3 = (f32[128,768]{1,0:T(8,128)}, f32[128,768]{1,0:T(8,128)S(1)}, u32[]{:S(2)}) copy-start(f32[128,768]{1,0:T(8,128)S(1)} %get-tuple-element.133.res_grad) | copy-start | bytes 1179652
  412.4 2.1 copy-start.6
  414.3 8.8 %slice-start = ((s8[4718592]{0:T(1024)(128)(4,1)}), s8[524288]{0:T(1024)(128)(4,1)S(1)}, s32[]{:S(2)}) async-start(s8[4718592]{0:T(1024)(128)(4,1)} %bitcast.118), calls=%async_computation.14 | async-start | bytes 1048576
  414.6 4.4 copy-start.9
  414.6 8.5 %slice-start.1 = ((s8[4718592]{0:T(1024)(128)(4,1)}), s8[4194304]{0:T(1024)(128)(4,1)S(1)}, s32[]{:S(2)}) async-start(s8[4718592]{0:T(1024)(128)(4,1)} %bitcast.118), calls=%async_computation.15 | async-start | bytes 8388608
  427.4 6.7 %copy-start.4 = (bf16[768,768]{1,0:T(8,128)(2,1)S(1)}, bf16[768,768]{1,0:T(8,128)(2,1)}, u32[]{:S(2)}) copy-start(bf16[768,768]{1,0:T(8,128)(2,1)} %all-gather.5.cloned.1.call-done) | copy-start | bytes 3538948
Sparse Core Ops, SparseCore 0:
  10.9 61.4 all-gather.4
  85.5 51.4 all-gather.6
  139.2 51.9 all-gather.8
  202.1 74.0 reduce-scatter.4
  280.9 74.5 reduce-scatter.6
  358.9 59.5 all-gather.10
  424.4 98.0 reduce-scatter.8
